TPU v7x, 256 devices: a whole 4x4x8 slice. The times are simulated.
256 devices in a mesh: ep: 64 (over z, y, core), tp: 4 (over x).
Axes of the slice: x: 4, y: 4, z: 8, core: 2. Of those that a mesh axis runs over, the one named last changes fastest.
Arguments:
- tokens: bfloat16 [8192, 4096], P(('ep', 'tp')), may hold values from -6 to 6
- grad_out: bfloat16 [8192, 4096], P(('ep', 'tp')), may hold values from -1 to 1
- expert_ids: int32 [8192, 3], P('ep'), may hold values from 0 to 63, all different within a row; in each aligned block of 32 rows (0 to 31, 32 to 63, ...) at most 2 rows name the same one
- gate_weights: bfloat16 [8192, 3], P('ep'), may hold values from 0.049804688 to 0.5
- w_gate: bfloat16 [64, 4096, 1536], P('ep', None, 'tp'), may hold values from -0.09375 to 0.09375
- w_up: bfloat16 [64, 4096, 1536], P('ep', None, 'tp'), may hold values from -0.09375 to 0.09375
- w_down: bfloat16 [64, 1536, 4096], P('ep', 'tp'), may hold values from -0.15625 to 0.15625
- scale_gate: float32 [64, 32, 12], P('ep', None, 'tp'), may hold values from 0.25 to 2
- scale_up: float32 [64, 32, 12], P('ep', None, 'tp'), may hold values from 0.25 to 2
- scale_down: float32 [64, 12, 32], P('ep', 'tp'), may hold values from 0.25 to 2
Outputs:
- grad_tokens: bfloat16 [8192, 4096], P(('ep', 'tp'))
- grad_gates: float32 [8192, 3], P(('ep', 'tp'))
Inputs may be any that keep to these rules, and one draw needn't show every extreme that they name: `expert_ids`: the 3 experts of a row are different. Within each aligned block of 32 rows no expert is named more than 2 times, and in some block one expert is named exactly 2 times.
All inputs are finite; a program needn't handle non-finite values.
Results may differ from a plain program's by a relative error of at most 0.018.
Values may be sent and summed in bfloat16 or wider, within the bound.
No kernel may reach another device: no remote copies, remote signals or barrier semaphores. Data moves between devices by JAX's collectives and lax.ppermute only.
A program may use at most 128 MiB of HBM per device.

v0:
```python
import jax
import jax.numpy as jnp
from jax import lax
from jax.sharding import PartitionSpec as P


def dequantize(quant, scales, block_side):
    rows, cols = quant.shape
    blocks = quant.astype(jnp.float32).reshape(
        rows // block_side, block_side, cols // block_side, block_side
    )
    return (blocks * scales[:, None, :, None]).reshape(rows, cols).astype(jnp.bfloat16)


def fill_slots(slot, pair_count, top_count, slot_count, rows_in, rows_dy, gate_flat):
    source = (
        jnp.zeros((slot_count,), jnp.int32)
        .at[slot]
        .set(jnp.arange(pair_count, dtype=jnp.int32) + 1)
    )
    filled = source > 0
    pair_pick = jnp.maximum(source - 1, 0)
    row_pick = pair_pick // top_count
    blank = jnp.zeros((), jnp.bfloat16)
    send_in = jnp.where(filled[:, None], rows_in[row_pick], blank)
    send_dy = jnp.where(filled[:, None], rows_dy[row_pick], blank)
    send_gate = jnp.where(filled, gate_flat[pair_pick], blank)
    return (send_in, send_dy, send_gate)


def shards(
    tokens,
    grad_out,
    expert_ids,
    gate_weights,
    w_gate,
    w_up,
    w_down,
    scale_gate,
    scale_up,
    scale_down,
):
    n_ep = lax.axis_size("ep")
    n_tp = lax.axis_size("tp")
    group_rows = expert_ids.shape[0]
    top_count = expert_ids.shape[1]
    width = tokens.shape[1]
    local_rows = group_rows // n_tp
    block_side = w_gate.shape[1] // scale_gate.shape[1]
    hid_local = w_gate.shape[2]
    experts = n_ep * w_gate.shape[0]
    cap_quarter = 3 * local_rows * top_count // (2 * experts)
    capacity = n_tp * cap_quarter
    expert_range = jnp.arange(experts, dtype=jnp.int32)
    wboth = jnp.concatenate(
        [
            dequantize(w_gate[0], scale_gate[0], block_side),
            dequantize(w_up[0], scale_up[0], block_side),
        ],
        axis=1,
    )
    wdown = dequantize(w_down[0], scale_down[0], block_side)
    rows_in, rows_dy = (
        lax.all_gather(tokens, "tp", axis=0, tiled=True),
        lax.all_gather(grad_out, "tp", axis=0, tiled=True),
    )
    flat_ids = expert_ids.reshape(-1)
    onehot = (flat_ids[:, None] == expert_range[None, :]).astype(jnp.int32)
    rank = jnp.sum(jnp.cumsum(onehot, axis=0) * onehot, axis=1) - 1
    slot = flat_ids * capacity + rank
    send_in, send_dy, send_gate = fill_slots(
        slot,
        group_rows * top_count,
        top_count,
        experts * capacity,
        rows_in,
        rows_dy,
        gate_weights.reshape(-1),
    )
    send_in = send_in.reshape(experts, capacity, width)
    send_dy = send_dy.reshape(experts, capacity, width)
    send_gate = send_gate.reshape(experts, capacity)
    recv_in = lax.all_to_all(send_in, "ep", split_axis=0, concat_axis=0, tiled=True)
    recv_dy = lax.all_to_all(send_dy, "ep", split_axis=0, concat_axis=0, tiled=True)
    recv_gate = lax.all_to_all(send_gate, "ep", split_axis=0, concat_axis=0, tiled=True)
    sources = recv_in.shape[0]
    count = recv_in.shape[1]
    flat_in = recv_in.reshape(sources * count, width)
    flat_dy = recv_dy.reshape(sources * count, width)
    both = jnp.dot(flat_in, wboth, preferred_element_type=jnp.float32)
    pre = both[:, :hid_local]
    upper = both[:, hid_local:]
    raw = lax.dot_general(
        flat_dy, wdown, (((1,), (1,)), ((), ())), preferred_element_type=jnp.float32
    )
    sig = jax.nn.sigmoid(pre)
    act = pre * sig
    hidden = act * upper
    part_gate = jnp.sum(hidden * raw, axis=1).astype(jnp.bfloat16)
    d_hidden = recv_gate.reshape(-1).astype(jnp.float32)[:, None] * raw
    d_upper = (d_hidden * act).astype(jnp.bfloat16)
    d_pre = (d_hidden * upper * sig * (1.0 + pre * (1.0 - sig))).astype(jnp.bfloat16)
    d_both = jnp.concatenate([d_pre, d_upper], axis=1)
    part_tok = lax.dot_general(
        d_both, wboth, (((1,), (1,)), ((), ())), preferred_element_type=jnp.float32
    )
    back_tok = lax.all_to_all(
        part_tok.astype(jnp.bfloat16).reshape(sources, count, width),
        "ep",
        split_axis=0,
        concat_axis=0,
        tiled=True,
    )
    back_gate = lax.all_to_all(
        part_gate.reshape(sources, count), "ep", split_axis=0, concat_axis=0, tiled=True
    )
    pair_tok = (
        back_tok.reshape(experts * capacity, width)[slot]
        .astype(jnp.float32)
        .reshape(group_rows, top_count, width)
    )
    token_part = jnp.sum(pair_tok, axis=1)
    gate_part = back_gate.reshape(-1)[slot].astype(jnp.float32).reshape(group_rows, top_count)
    grad_rows, grad_gates = (
        lax.psum_scatter(
            token_part.astype(jnp.bfloat16), "tp", scatter_dimension=0, tiled=True
        ).astype(jnp.float32),
        lax.psum_scatter(
            gate_part.astype(jnp.bfloat16), "tp", scatter_dimension=0, tiled=True
        ).astype(jnp.float32),
    )
    return (grad_rows.astype(jnp.bfloat16), grad_gates)


def solution(mesh):
    return jax.shard_map(
        shards,
        mesh=mesh,
        in_specs=(
            P(("ep", "tp"), None),
            P(("ep", "tp"), None),
            P("ep", None),
            P("ep", None),
            P("ep", None, "tp"),
            P("ep", None, "tp"),
            P("ep", "tp", None),
            P("ep", None, "tp"),
            P("ep", None, "tp"),
            P("ep", "tp", None),
        ),
        out_specs=(P(("ep", "tp"), None), P(("ep", "tp"), None)),
        check_vma=False,
    )
```

profile of v0, /device:TPU:8, one launch (start us, length us, event | category | flops | bytes accessed | tf_op | source)
XLA Modules:
  0.0 471.8 jit_solution(16147681917136757586)
XLA Ops:
  13.2 2.9 scatter_custom_fusion
  16.2 3.5 gather_fusion
  20.4 12.1 %all-to-all-start = ((bf16[64,1,8]{2,1,0:T(2,128)(2,1)}), bf16[64,1,8]{2,1,0:T(2,128)(2,1)S(1)}, u32[]{:S(2)}, u32[]{:S(2)}) async-start(bf16[64,1,8]{2,1,0:T(2,128)(2,1)} %all_to_all.25), calls=%async_computation | async-start | bytes 65536 | tf_op jit(solution)/shard_map/all_to_all | solution.py:85
  32.7 6.5 %all-gather.5.cloned.1.call-done = bf16[128,4096]{1,0:T(8,128)(2,1)} async-done(((bf16[32,4096]{1,0:T(8,128)(2,1)}), bf16[128,4096]{1,0:T(8,128)(2,1)}) %all-gather.5.cloned.1.call-update) | async-done | bytes 1048592 | tf_op jit(solution)/shard_map/all_gather | solution.py:64
  39.2 10.0 %gather_fusion.2 = bf16[512,4096]{1,0:T(8,128)(2,1)} fusion(bf16[128,4096]{1,0:T(8,128)(2,1)} %all-gather.5.cloned.1.call-done, s32[1024]{0:T(1024)S(1)} %pad_clamp_fusion.1), kind=kCustom, calls=%fused_computation.2 | custom fusion | bytes 8390656 | tf_op jit(solution)/shard_map/gather | solution.py:25
  49.2 18.7 %all-gather.3.cloned.1.call-done = bf16[128,4096]{1,0:T(8,128)(2,1)} async-done(((bf16[32,4096]{1,0:T(8,128)(2,1)}), bf16[128,4096]{1,0:T(8,128)(2,1)}) %all-gather.3.cloned.1.call-update) | async-done | bytes 1048592 | tf_op jit(solution)/shard_map/all_gather | solution.py:65
  67.9 9.9 %gather_fusion.1 = bf16[512,4096]{1,0:T(8,128)(2,1)} fusion(bf16[128,4096]{1,0:T(8,128)(2,1)} %all-gather.3.cloned.1.call-done, s32[1024]{0:T(1024)S(1)} %pad_clamp_fusion.1), kind=kCustom, calls=%fused_computation.1 | custom fusion | bytes 8390656 | tf_op jit(solution)/shard_map/gather | solution.py:26
  77.8 5.8 %bitcast_select_fusion = (bf16[64,8,4096]{2,1,0:T(8,128)(2,1)}, bf16[64,8,4096]{2,1,0:T(8,128)(2,1)}) fusion(bf16[512,4096]{1,0:T(8,128)(2,1)} %gather_fusion.2, pred[64,8]{1,0:T(8,128)(4,1)S(1)} %broadcast_in_dim.38, bf16[512,4096]{1,0:T(8,128)(2,1)} %gather_fusion.1), kind=kLoop, calls=%fused_computation.18 | loop fusion | flops 4194304 | bytes 16777728 | tf_op jit(solution)/shard_map/jit(_where)/select_n | solution.py:25
  83.7 107.3 %all_to_all.31 = bf16[64,8,4096]{2,1,0:T(8,128)(2,1)} all-to-all(bf16[64,8,4096]{2,1,0:T(8,128)(2,1)} %get-tuple-element.11), channel_id=1, replica_groups=mesh['ep'=64,'tp'=4] {'ep'}, dimensions={0} | all-to-all | bytes 8388608 | tf_op jit(solution)/shard_map/all_to_all | solution.py:83
  191.0 5.8 %all-to-all-start.1 = ((bf16[64,8,4096]{2,1,0:T(8,128)(2,1)}), bf16[64,8,4096]{2,1,0:T(8,128)(2,1)}, u32[]{:S(2)}, u32[]{:S(2)}) async-start(bf16[64,8,4096]{2,1,0:T(8,128)(2,1)} %get-tuple-element.12), calls=%async_computation.1 | async-start | bytes 8388608 | tf_op jit(solution)/shard_map/all_to_all | solution.py:84
  196.8 3.2 copy.33
  200.0 4.7 copy.32
  214.0 10.2 %fusion = (bf16[4096,384]{0,1:T(8,128)(2,1)}, bf16[4096,384]{0,1:T(8,128)(2,1)}) fusion(f32[48,8,32,128]{3,2,1,0:T(8,128)S(1)} %bitcast.79, bf16[1,4096,384]{1,2,0:T(8,128)(2,1)S(1)} %copy.33, f32[48,8,32,128]{3,2,1,0:T(8,128)S(1)} %bitcast.80, bf16[1,4096,384]{1,2,0:T(8,128)(2,1)S(1)} %copy-done), kind=kLoop, calls=%fused_computation.7 | loop fusion | flops 9437184 | bytes 25165824 | tf_op jit(solution)/shard_map/convert_element_type | solution.py:12
  224.4 8.7 %fusion.4 = f32[512,768]{0,1:T(8,128)} fusion(bf16[64,8,4096]{2,1,0:T(8,128)(2,1)} %all_to_all.31, bf16[4096,384]{0,1:T(8,128)(2,1)} %get-tuple-element.15, bf16[4096,384]{0,1:T(8,128)(2,1)} %get-tuple-element.16), kind=kOutput, calls=%fused_computation.16 | convolution fusion | flops 3233808384 | bytes 12058624 | tf_op jit(solution)/shard_map/dot_general | solution.py:90
  233.1 59.9 %all-to-all-done.1 = bf16[64,8,4096]{2,1,0:T(8,128)(2,1)} async-done(((bf16[64,8,4096]{2,1,0:T(8,128)(2,1)}), bf16[64,8,4096]{2,1,0:T(8,128)(2,1)}, u32[]{:S(2)}, u32[]{:S(2)}) %all-to-all-start.1) | async-done | bytes 4194336 | tf_op jit(solution)/shard_map/all_to_all | solution.py:84
  293.0 6.8 %multiply_convert_fusion.1 = (bf16[512,384]{0,1:T(8,128)(2,1)}, bf16[512,384]{0,1:T(8,128)(2,1)}, bf16[512]{0:T(512)(128)(2,1)S(1)}) fusion(f32[512,768]{0,1:T(8,128)} %fusion.4, f32[512]{0:T(512)S(1)} %reshape.165, bf16[48,8,32,128]{3,2,1,0:T(8,128)(2,1)} %bitcast.81, bf16[64,8,4096]{2,1,0:T(8,128)(2,1)} %all-to-all-done.1), kind=kOutput, calls=%fused_computation.29 | convolution fusion | flops 1613954560 | bytes 9702400 | tf_op jit(solution)/shard_map/dot_general | solution.py:93
  300.5 5.4 %all-to-all-start.4 = ((bf16[64,1,8]{2,1,0:T(2,128)(2,1)}), bf16[64,1,8]{2,1,0:T(2,128)(2,1)S(1)}, u32[]{:S(2)}, u32[]{:S(2)}) async-start(bf16[64,1,8]{2,1,0:T(2,128)(2,1)} %convert_element_type.121), calls=%async_computation.5 | async-start | bytes 65536 | tf_op jit(solution)/shard_map/all_to_all | solution.py:114
  306.0 7.5 %fusion.3 = bf16[64,8,4096]{2,1,0:T(8,128)(2,1)} fusion(bf16[4096,384]{0,1:T(8,128)(2,1)S(1)} %copy-done.1, bf16[4096,384]{0,1:T(8,128)(2,1)} %get-tuple-element.16, bf16[512,384]{0,1:T(8,128)(2,1)} %get-tuple-element.9, bf16[512,384]{0,1:T(8,128)(2,1)} %get-tuple-element.8), kind=kOutput, calls=%fused_computation.15 | convolution fusion | flops 3237478400 | bytes 11272192 | tf_op jit(solution)/shard_map/dot_general | solution.py:104
  314.5 9.5 %all-to-all-start.3 = ((bf16[64,8,4096]{2,1,0:T(8,128)(2,1)}), bf16[64,8,4096]{2,1,0:T(8,128)(2,1)}, u32[]{:S(2)}, u32[]{:S(2)}) async-start(bf16[64,8,4096]{2,1,0:T(8,128)(2,1)} %fusion.3), calls=%async_computation.3 | async-start | bytes 8388608 | tf_op jit(solution)/shard_map/all_to_all | solution.py:107
  328.0 92.1 %all-to-all-done.3 = bf16[64,8,4096]{2,1,0:T(8,128)(2,1)} async-done(((bf16[64,8,4096]{2,1,0:T(8,128)(2,1)}), bf16[64,8,4096]{2,1,0:T(8,128)(2,1)}, u32[]{:S(2)}, u32[]{:S(2)}) %all-to-all-start.3) | async-done | bytes 4194336 | tf_op jit(solution)/shard_map/all_to_all | solution.py:107
  420.1 10.4 %gather_fusion.3 = bf16[384,4096]{1,0:T(8,128)(2,1)S(1)} fusion(bf16[512,4096]{1,0:T(8,128)(2,1)} %bitcast.8, s32[1024]{0:T(1024)S(1)} %pad_clamp_fusion), kind=kCustom, calls=%fused_computation.3 | custom fusion | bytes 6292992 | tf_op jit(solution)/shard_map/gather | solution.py:118
  430.6 4.4 gather.29
  435.0 8.5 %reduce_sum.31 = bf16[128,4096]{1,0:T(8,128)(2,1)} reduce(bf16[128,3,4096]{2,1,0:T(4,128)(2,1)} %gather.29, bf16[]{:T(256)} %constant.32.clone.1), dimensions={1}, to_apply=%region_4.5 | reduce | flops 1048576 | bytes 4194306 | tf_op jit(solution)/shard_map/reduce_sum | solution.py:122
  444.9 20.1 %reduce-scatter.3.cloned.1.call-done = bf16[32,4096]{1,0:T(8,128)(2,1)} async-done(((bf16[128,4096]{1,0:T(8,128)(2,1)}), bf16[32,4096]{1,0:T(8,128)(2,1)}) %reduce-scatter.3.cloned.1.call-update) | async-done | bytes 262160 | tf_op jit(solution)/shard_map/reduce_scatter | solution.py:125
  (60 shorter events, 23.3 us)
Async XLA Ops:
  7.2 32.1 %all-gather.5.cloned.1.call-start = ((), (), s32[]{:S(2)}) async-start(), calls=%async_computation.8 | async-start | bytes 1310720 | tf_op jit(solution)/shard_map/all_gather | solution.py:64
  7.9 60.0 %all-gather.3.cloned.1.call-start = ((), (), s32[]{:S(2)}) async-start(), calls=%async_computation.7 | async-start | bytes 1310720 | tf_op jit(solution)/shard_map/all_gather | solution.py:65
  20.4 63.2 %all-to-all-start = ((bf16[64,1,8]{2,1,0:T(2,128)(2,1)}), bf16[64,1,8]{2,1,0:T(2,128)(2,1)S(1)}, u32[]{:S(2)}, u32[]{:S(2)}) async-start(bf16[64,1,8]{2,1,0:T(2,128)(2,1)} %all_to_all.25), calls=%async_computation | async-start | bytes 65536 | tf_op jit(solution)/shard_map/all_to_all | solution.py:85
  191.0 5.8 %copy-start.2 = (f32[1,32,3]{1,0,2:T(1,128)S(1)}, f32[1,32,3]{1,0,2:T(1,128)}, u32[]{:S(2)}) copy-start(f32[1,32,3]{1,0,2:T(1,128)} %param.18) | copy-start | bytes 1156
  191.0 102.0 %all-to-all-start.1 = ((bf16[64,8,4096]{2,1,0:T(8,128)(2,1)}), bf16[64,8,4096]{2,1,0:T(8,128)(2,1)}, u32[]{:S(2)}, u32[]{:S(2)}) async-start(bf16[64,8,4096]{2,1,0:T(8,128)(2,1)} %get-tuple-element.12), calls=%async_computation.1 | async-start | bytes 8388608 | tf_op jit(solution)/shard_map/all_to_all | solution.py:84
  196.8 3.2 copy-start.3
  200.0 4.7 %copy-start.4 = (f32[1,3,32]{2,0,1:T(1,128)S(1)}, f32[1,3,32]{2,0,1:T(1,128)}, u32[]{:S(2)}) copy-start(f32[1,3,32]{2,0,1:T(1,128)} %param.19) | copy-start | bytes 1156
  212.1 1.9 copy-start
  293.0 13.0 %copy-start.1 = (bf16[4096,384]{0,1:T(8,128)(2,1)S(1)}, bf16[4096,384]{0,1:T(8,128)(2,1)}, u32[]{:S(2)}) copy-start(bf16[4096,384]{0,1:T(8,128)(2,1)} %get-tuple-element.15) | copy-start | bytes 9437188
  300.5 14.0 %all-to-all-start.4 = ((bf16[64,1,8]{2,1,0:T(2,128)(2,1)}), bf16[64,1,8]{2,1,0:T(2,128)(2,1)S(1)}, u32[]{:S(2)}, u32[]{:S(2)}) async-start(bf16[64,1,8]{2,1,0:T(2,128)(2,1)} %convert_element_type.121), calls=%async_computation.5 | async-start | bytes 65536 | tf_op jit(solution)/shard_map/all_to_all | solution.py:114
  314.5 105.6 %all-to-all-start.3 = ((bf16[64,8,4096]{2,1,0:T(8,128)(2,1)}), bf16[64,8,4096]{2,1,0:T(8,128)(2,1)}, u32[]{:S(2)}, u32[]{:S(2)}) async-start(bf16[64,8,4096]{2,1,0:T(8,128)(2,1)} %fusion.3), calls=%async_computation.3 | async-start | bytes 8388608 | tf_op jit(solution)/shard_map/all_to_all | solution.py:107
  324.0 119.6 %reduce-scatter.5.cloned.1.call-start = ((), (), s32[]{:S(2)}) async-start(), calls=%async_computation.10 | async-start | bytes 40960 | tf_op jit(solution)/shard_map/reduce_scatter | solution.py:128
  327.9 137.1 %reduce-scatter.3.cloned.1.call-start = ((), (), s32[]{:S(2)}) async-start(), calls=%async_computation.9 | async-start | bytes 1310720 | tf_op jit(solution)/shard_map/reduce_scatter | solution.py:125
Sparse Core Ops, SparseCore 0:
  9.8 29.3 all-gather.4
  41.0 26.8 all-gather.2
  328.1 22.8 reduce-scatter.4
  443.7 21.2 reduce-scatter.2
where the time goes:
time: 481 us; the launch traced here: 472 us
  waiting for transfers between devices  200 us (42%)
  blocking collectives  107 us (22%)
  local copies, waits for them, and re-layouts  62.6 us (13%)
  starting transfers between devices  33 us (7%)
  other arithmetic  31.8 us (7%)
  matrix products  23.1 us (5%)
  between operations  14.3 us (3%)
    all_to_all x1, blocking collectives, shards(): lax.all_to_all(send_in, 'ep', split_axis=0, concat_axis=0, tiled=True)  107 us
    all_to_all x1, waiting for transfers between devices, shards(): lax.all_to_all(part_tok.astype(jnp.bfloat16).reshape(sources, count, widt...  92.1 us
    all_to_all x1, waiting for transfers between devices, shards(): lax.all_to_all(send_dy, 'ep', split_axis=0, concat_axis=0, tiled=True)  59.9 us
    reduce_scatter x1, waiting for transfers between devices, shards(): lax.psum_scatter(token_part.astype(jnp.bfloat16), 'tp', scatter_dimension...  20.1 us
    all_gather x1, waiting for transfers between devices, shards(): lax.all_gather(grad_out, 'tp', axis=0, tiled=True)  18.7 us
    gather x2, local copies, waits for them, and re-layouts, shards(): back_tok.reshape(experts * capacity, width)[slot].astype(jnp.float32)  14.9 us
    unnamed x19, local copies, waits for them, and re-layouts  13.2 us
    convert_element_type x2, other arithmetic, dequantize(): (blocks * scales[:, None, :, None]).reshape(rows, cols).astype(jnp.bfloat16)  12.8 us
  transfers between devices with their start and end apart: 8, of which 6 were waited for; matrix products, arithmetic and copies ran while one was open for 23% of the time, Pallas kernels for 0%

commit v1 on v0

v1 whole, which is shorter than its diff:
```python
import functools

import jax
import jax.numpy as jnp
from jax import lax
from jax.experimental import pallas as pl
from jax.experimental.pallas import tpu as pltpu
from jax.sharding import PartitionSpec as P

BF = jnp.bfloat16
F32 = jnp.float32
BLOCK = 128
MIB = 1 << 20
VMEM = pl.BlockSpec(memory_space=pltpu.VMEM)
SMEM = pl.BlockSpec(memory_space=pltpu.SMEM)


def params(mib):
    return pltpu.CompilerParams(vmem_limit_bytes=mib * MIB)


def cost(flops, moved):
    return pl.CostEstimate(flops=flops, bytes_accessed=moved, transcendentals=0)


def dot(a, b, dims=((1,), (0,))):
    return lax.dot_general(a, b, (dims, ((), ())), preferred_element_type=F32)


def pack_kernel(rows, t_ref, ids_ref, gates_ref, x_ref, d_ref, sx_ref, sd_ref, comb_ref, pick_ref):
    t = t_ref[0]
    top, group = ids_ref.shape
    slots = sx_ref.shape[0]
    width = x_ref.shape[1]
    lane = lax.broadcasted_iota(jnp.int32, (slots, group), 0)
    row = lax.broadcasted_iota(jnp.int32, (slots, group), 1)
    expert, copy = lane // 2, lane % 2
    mine = (row // rows) == t
    hits = [(ids_ref[k : k + 1, :] == expert) & mine for k in range(top)]
    member = functools.reduce(jnp.logical_or, hits)
    member = jnp.where(member, 1.0, 0.0).astype(BF)
    before = lax.broadcasted_iota(jnp.int32, (group, group), 0) < lax.broadcasted_iota(
        jnp.int32, (group, group), 1
    )
    prior = dot(member, jnp.where(before, 1.0, 0.0).astype(BF))
    ranked = prior == copy.astype(F32)
    keep = lax.broadcasted_iota(jnp.int32, (group, rows), 0) == t * rows + lax.broadcasted_iota(
        jnp.int32, (group, rows), 1
    )
    keep = jnp.where(keep, 1.0, 0.0).astype(BF)
    weight = jnp.zeros((slots, group), F32)
    send = jnp.zeros((slots, rows), F32)
    for k in range(top):
        hit = jnp.where(hits[k] & ranked, 1.0, 0.0)
        weight = weight + hit * gates_ref[k : k + 1, :].astype(F32)
        picked = dot(hit.astype(BF), keep)
        pick_ref[k] = picked.astype(BF)
        send = send + picked
    comb_ref[...] = dot(keep, weight.astype(BF), ((0,), (1,))).astype(BF)
    send = send.astype(BF)
    step = 1024
    for c in range(0, width, step):
        sx_ref[:, c : c + step] = dot(send, x_ref[:, c : c + step]).astype(BF)
    for c in range(0, width, step):
        sd_ref[:, c : c + step] = dot(send, d_ref[:, c : c + step]).astype(BF)


def prep_kernel(sg_ref, su_ref, sd_ref, wg_ref, wu_ref, wd_ref, both_ref, back_ref, down_ref):
    i = pl.program_id(0)
    depth, hid = wg_ref.shape
    for b in range(depth // BLOCK):
        at = i * (depth // BLOCK) + b
        rs = slice(b * BLOCK, (b + 1) * BLOCK)
        for j in range(hid // BLOCK):
            cs = slice(j * BLOCK, (j + 1) * BLOCK)
            ct = slice(hid + j * BLOCK, hid + (j + 1) * BLOCK)
            g = wg_ref[rs, cs].astype(F32) * sg_ref[at, j]
            u = wu_ref[rs, cs].astype(F32) * su_ref[at, j]
            d = wd_ref[cs, rs].astype(F32) * sd_ref[j, at]
            both_ref[rs, cs] = g.astype(BF)
            both_ref[rs, ct] = u.astype(BF)
            back_ref[cs, rs] = g.T.astype(BF)
            back_ref[ct, rs] = u.T.astype(BF)
            down_ref[rs, cs] = d.T.astype(BF)


def joined(refs):
    return jnp.concatenate([r[...] for r in refs], axis=0)


def forward_kernel(*refs):
    pieces, w_ref, out_ref = refs[:8], refs[8], refs[9]
    part = dot(joined(pieces), w_ref[...])

    @pl.when(pl.program_id(0) == 0)
    def _():
        out_ref[...] = part

    @pl.when(pl.program_id(0) > 0)
    def _():
        out_ref[...] += part


def middle_kernel(*refs):
    pieces, w_ref, pre_ref, d_ref, gate_ref, raw_ref = refs[:8], *refs[8:]
    part = dot(joined(pieces), w_ref[...])

    @pl.when(pl.program_id(0) == 0)
    def _():
        raw_ref[...] = part

    @pl.when(pl.program_id(0) > 0)
    def _():
        raw_ref[...] += part

    @pl.when(pl.program_id(0) == pl.num_programs(0) - 1)
    def _():
        hid = raw_ref.shape[1]
        step = 128
        for r in range(0, raw_ref.shape[0], step):
            rs = slice(r, r + step)
            raw = raw_ref[rs, :]
            pre = pre_ref[rs, :hid]
            up = pre_ref[rs, hid:]
            sig = 1.0 / (1.0 + jnp.exp(-pre))
            act = pre * sig
            total = jnp.sum(act * up * raw, axis=1, keepdims=True)
            d_ref[rs, hid:] = (raw * act).astype(BF)
            d_ref[rs, :hid] = (raw * up * sig * (1.0 + pre * (1.0 - sig))).astype(BF)
            col = lax.broadcasted_iota(jnp.int32, (step, BLOCK), 1)
            gate_ref[rs, :] = jnp.where(col == 0, total, 0.0).astype(BF)


def backward_kernel(has_gate, *refs):
    d_ref, w_ref = refs[:2]
    outs = refs[3:] if has_gate else refs[2:]
    own, rest = outs[0], outs[1:]
    width = w_ref.shape[1]
    step = 512

    def put(rows, cs, value):
        if rows < 128:
            own[rows : rows + 64, cs] = value
        else:
            rest[rows // 64 - 2][:, cs] = value

    for c in range(0, width, step):
        cs = slice(c, c + step)
        part = dot(d_ref[...], w_ref[:, cs]).astype(BF)
        for r in range(0, 512, 64):
            put(r, cs, part[r : r + 64])
    if has_gate:
        cs = slice(width, width + BLOCK)
        for r in range(0, 512, 64):
            put(r, cs, refs[2][r : r + 64, :])


def combine_kernel(comb_ref, pick_ref, *refs):
    backs, tok_ref, gate_ref = refs[:-2], refs[-2], refs[-1]
    at = 0
    comb = comb_ref[...]
    for b in backs:
        width = min(b.shape[1], tok_ref.shape[1] - at)
        tok_ref[:, at : at + width] = dot(comb, b[:, :width]).astype(BF)
        at += width
    sums = backs[-1][:, backs[-1].shape[1] - BLOCK :]
    for k in range(pick_ref.shape[0]):
        gate_ref[k : k + 1, :] = dot(sums, pick_ref[k], ((0,), (0,)))[:1, :]


def ring(n, by):
    return [(i, (i + by) % n) for i in range(n)]


def gather_pieces(x, n):
    h = x.shape[0] // 2
    x1, x2 = x[:h], x[h:]
    right = lambda v: lax.ppermute(v, "tp", ring(n, 1))
    left = lambda v: lax.ppermute(v, "tp", ring(n, -1))
    l1, r2 = right(x1), left(x2)
    l2, r1 = right(x2), left(x1)
    o1, o2 = right(l1), left(r2)
    return [x1, x2, l1, l2, r1, r2, o1, o2]


def scatter_sum(pieces, n):
    own, l1, l2, r1, r2, o1, o2 = pieces
    right = lambda v: lax.ppermute(v, "tp", ring(n, 1))
    left = lambda v: lax.ppermute(v, "tp", ring(n, -1))
    a, b = right(o1), left(o2)
    c2, e1 = right(r2), left(l1)
    c1 = right((r1.astype(F32) + a.astype(F32)).astype(BF))
    e2 = left((l2.astype(F32) + b.astype(F32)).astype(BF))
    h = own.shape[0] // 2
    first = own[:h].astype(F32) + c1.astype(F32) + e1.astype(F32)
    second = own[h:].astype(F32) + c2.astype(F32) + e2.astype(F32)
    return jnp.concatenate([first, second], axis=0).astype(BF)


def exchange(x, experts):
    slots, width = x.shape
    y = lax.all_to_all(
        x.reshape(experts, slots // experts, width), "ep", split_axis=0, concat_axis=0, tiled=True
    )
    return y.reshape(slots, width)


def shards(tokens, grad_out, expert_ids, gate_weights, w_gate, w_up, w_down, scale_gate, scale_up, scale_down):
    n_tp = lax.axis_size("tp")
    experts = lax.axis_size("ep")
    rows, width = tokens.shape
    top = expert_ids.shape[1]
    hid = w_gate.shape[2]
    slots = 2 * experts
    total = n_tp * slots
    t = lax.axis_index("tp").astype(jnp.int32).reshape(1)

    send_in, send_dy, comb, pick = pl.pallas_call(
        functools.partial(pack_kernel, rows),
        in_specs=[SMEM, VMEM, VMEM, VMEM, VMEM],
        out_specs=[VMEM] * 4,
        out_shape=[
            jax.ShapeDtypeStruct((slots, width), BF),
            jax.ShapeDtypeStruct((slots, width), BF),
            jax.ShapeDtypeStruct((rows, slots), BF),
            jax.ShapeDtypeStruct((top, slots, rows), BF),
        ],
        compiler_params=params(24),
        cost_estimate=cost(4 * slots * rows * width, 6 * slots * width),
        name="pack",
    )(t, expert_ids.T, gate_weights.T, tokens, grad_out)

    depth = 512
    steps = width // depth
    both, back, down = pl.pallas_call(
        prep_kernel,
        grid=(steps,),
        in_specs=[
            SMEM,
            SMEM,
            SMEM,
            pl.BlockSpec((depth, hid), lambda i: (i, 0)),
            pl.BlockSpec((depth, hid), lambda i: (i, 0)),
            pl.BlockSpec((hid, depth), lambda i: (0, i)),
        ],
        out_specs=[
            pl.BlockSpec((depth, 2 * hid), lambda i: (i, 0)),
            pl.BlockSpec((2 * hid, depth), lambda i: (0, i)),
            pl.BlockSpec((depth, hid), lambda i: (i, 0)),
        ],
        out_shape=[
            jax.ShapeDtypeStruct((width, 2 * hid), BF),
            jax.ShapeDtypeStruct((2 * hid, width), BF),
            jax.ShapeDtypeStruct((width, hid), BF),
        ],
        compiler_params=params(24),
        cost_estimate=cost(8 * width * hid, 16 * width * hid),
        name="prep",
    )(scale_gate[0], scale_up[0], scale_down[0], w_gate[0], w_up[0], w_down[0])

    x_pieces = gather_pieces(exchange(send_in, experts), n_tp)
    d_pieces = gather_pieces(exchange(send_dy, experts), n_tp)

    piece_specs = [pl.BlockSpec((slots // 2, depth), lambda i: (0, i))] * 8
    pre_up = pl.pallas_call(
        forward_kernel,
        grid=(steps,),
        in_specs=piece_specs + [pl.BlockSpec((depth, 2 * hid), lambda i: (i, 0))],
        out_specs=pl.BlockSpec((total, 2 * hid), lambda i: (0, 0)),
        out_shape=jax.ShapeDtypeStruct((total, 2 * hid), F32),
        compiler_params=params(24),
        cost_estimate=cost(4 * total * width * hid, 4 * width * hid + 2 * total * width),
        name="forward",
    )(*x_pieces, both)

    d_both, part_gate = pl.pallas_call(
        middle_kernel,
        grid=(steps,),
        in_specs=piece_specs
        + [
            pl.BlockSpec((depth, hid), lambda i: (i, 0)),
            pl.BlockSpec((total, 2 * hid), lambda i: (0, 0)),
        ],
        out_specs=[
            pl.BlockSpec((total, 2 * hid), lambda i: (0, 0)),
            pl.BlockSpec((total, BLOCK), lambda i: (0, 0)),
        ],
        out_shape=[
            jax.ShapeDtypeStruct((total, 2 * hid), BF),
            jax.ShapeDtypeStruct((total, BLOCK), BF),
        ],
        scratch_shapes=[pltpu.VMEM((total, hid), F32)],
        compiler_params=params(24),
        cost_estimate=cost(2 * total * width * hid, 2 * width * hid + 2 * total * width),
        name="middle",
    )(*d_pieces, down, pre_up)

    cuts = 2
    part = width // cuts
    returned = []
    for c in range(cuts):
        has_gate = c == cuts - 1
        out_width = part + (BLOCK if has_gate else 0)
        shapes = [slots] + [slots // 2] * 6
        terms = pl.pallas_call(
            functools.partial(backward_kernel, has_gate),
            grid=(1,),
            in_specs=[
                pl.BlockSpec((total, 2 * hid), lambda i: (0, 0)),
                pl.BlockSpec((2 * hid, part), lambda i, c=c: (0, c)),
            ]
            + ([pl.BlockSpec((total, BLOCK), lambda i: (0, 0))] if has_gate else []),
            out_specs=[pl.BlockSpec((s, out_width), lambda i: (0, 0)) for s in shapes],
            out_shape=[jax.ShapeDtypeStruct((s, out_width), BF) for s in shapes],
            compiler_params=params(24),
            cost_estimate=cost(4 * total * part * hid, 4 * part * hid + 2 * total * part),
            name="backward",
        )(*([d_both, back] + ([part_gate] if has_gate else [])))
        returned.append(exchange(scatter_sum(terms, n_tp), experts))

    grad_rows, grad_gates = pl.pallas_call(
        combine_kernel,
        in_specs=[VMEM] * (2 + cuts),
        out_specs=[VMEM, VMEM],
        out_shape=[
            jax.ShapeDtypeStruct((rows, width), BF),
            jax.ShapeDtypeStruct((top, rows), F32),
        ],
        compiler_params=params(16),
        cost_estimate=cost(2 * slots * rows * width, 3 * slots * width),
        name="combine",
    )(comb, pick, *returned)
    return grad_rows, grad_gates.T


def solution(mesh):
    return jax.shard_map(
        shards,
        mesh=mesh,
        in_specs=(
            P(("ep", "tp"), None),
            P(("ep", "tp"), None),
            P("ep", None),
            P("ep", None),
            P("ep", None, "tp"),
            P("ep", None, "tp"),
            P("ep", "tp", None),
            P("ep", None, "tp"),
            P("ep", None, "tp"),
            P("ep", "tp", None),
        ),
        out_specs=(P(("ep", "tp"), None), P(("ep", "tp"), None)),
        check_vma=False,
    )
```

time: 481 us -> 234 us (0.49); the launches traced: 472 us -> 232 us
  blocking collectives: 107 us -> 0 us
  waiting for transfers between devices: 200 us -> 106 us
  starting transfers between devices: 33 us -> 68 us
  local copies, waits for them, and re-layouts: 62.6 us -> 27.9 us
  other arithmetic: 31.8 us -> 3.35 us
  Pallas kernels: 0 us -> 26 us
  matrix products: 23.1 us -> 0 us
  between operations: 14.3 us -> 0.93 us
    all_to_all x1 -> x0, blocking collectives: 107 us -> none  [shards(): lax.all_to_all(send_in, 'ep', split_axis=0, concat_axis=0, tiled=True)]
    all_to_all x4, waiting for transfers between devices: 153 us -> 76.2 us  [exchange(): lax.all_to_all(x.reshape(experts, slots // experts, width), 'ep', split_a...]
    gather x7 -> x0, local copies, waits for them, and re-layouts: 41.9 us -> none  [the longest x2 14.9 us: shards(): back_tok.reshape(experts * capacity, width)[slot].astype(jnp.float32)]
    ppermute x0 -> x24, starting transfers between devices: none -> 36.4 us  [the longest x6 13 us: scatter_sum(): left = lambda v: lax.ppermute(v, 'tp', ring(n, -1))]
    ppermute x0 -> x24, waiting for transfers between devices: none -> 29.6 us  [the longest x6 15.9 us: gather_pieces(): right = lambda v: lax.ppermute(v, 'tp', ring(n, 1))]
    pallas_call x0 -> x7, Pallas kernels: none -> 26 us  [the longest x1 7.75 us: shards(): pl.pallas_call(forward_kernel, grid=(steps,), in_specs=piece_specs + [pl....]
    all_gather x2 -> x0, waiting for transfers between devices: 25.3 us -> none  [the longest x1 18.7 us: shards(): lax.all_gather(grad_out, 'tp', axis=0, tiled=True)]
    dot_general x3 -> x0, matrix products: 23.1 us -> none  [the longest x1 8.71 us: shards(): both = jnp.dot(flat_in, wboth, preferred_element_type=jnp.float32)]
  transfers between devices with their start and end apart: 8 -> 28, of which waited for: 6 -> 14; matrix products, arithmetic and copies ran while one was open for 23% -> 9% of each run, Pallas kernels for 0% -> 6%
where the time goes in v1:
time: 234 us; the launch traced here: 232 us
  waiting for transfers between devices  106 us (45%)
  starting transfers between devices  68 us (29%)
  local copies, waits for them, and re-layouts  27.9 us (12%)
  Pallas kernels  26 us (11%)
  other arithmetic  3.35 us (1%)
    all_to_all x4, waiting for transfers between devices, exchange(): lax.all_to_all(x.reshape(experts, slots // experts, width), 'ep', split_a...  76.2 us
    all_to_all x4, starting transfers between devices, exchange(): lax.all_to_all(x.reshape(experts, slots // experts, width), 'ep', split_a...  31.6 us
    ppermute x6, waiting for transfers between devices, gather_pieces(): right = lambda v: lax.ppermute(v, 'tp', ring(n, 1))  15.9 us
    slice x6, local copies, waits for them, and re-layouts, gather_pieces(): x1, x2 = (x[:h], x[h:])  13.4 us
    ppermute x6, starting transfers between devices, scatter_sum(): left = lambda v: lax.ppermute(v, 'tp', ring(n, -1))  13 us
    ppermute x6, starting transfers between devices, gather_pieces(): left = lambda v: lax.ppermute(v, 'tp', ring(n, -1))  13 us
    unnamed x37, local copies, waits for them, and re-layouts  8.7 us
    pallas_call x1, Pallas kernels, shards(): pl.pallas_call(forward_kernel, grid=(steps,), in_specs=piece_specs + [pl....  7.75 us
  transfers between devices with their start and end apart: 28, of which 14 were waited for; matrix products, arithmetic and copies ran while one was open for 9% of the time, Pallas kernels for 6%

profile of v1, /device:TPU:8, one launch (start us, length us, event | category | flops | bytes accessed | tf_op | source)
XLA Modules:
  0.0 231.9 jit_solution(9814418235997515397)
XLA Ops:
  6.4 12.1 %all-to-all-start.1 = ((bf16[64,2,4096]{2,1,0:T(2,128)(2,1)}), bf16[64,2,4096]{2,1,0:T(2,128)(2,1)S(1)}, u32[]{:S(2)}, u32[]{:S(2)}) async-start(bf16[64,2,4096]{2,1,0:T(2,128)(2,1)} %reshape.33), calls=%async_computation.1 | async-start | bytes 2097152 | tf_op jit(solution)/shard_map/all_to_all | solution.py:202
  20.0 27.3 %all-to-all-done.1 = bf16[64,2,4096]{2,1,0:T(2,128)(2,1)S(1)} async-done(((bf16[64,2,4096]{2,1,0:T(2,128)(2,1)}), bf16[64,2,4096]{2,1,0:T(2,128)(2,1)S(1)}, u32[]{:S(2)}, u32[]{:S(2)}) %all-to-all-start.1) | async-done | bytes 1048608 | tf_op jit(solution)/shard_map/all_to_all | solution.py:202
  47.3 5.8 %all-to-all-start = ((bf16[64,2,4096]{2,1,0:T(2,128)(2,1)}), bf16[64,2,4096]{2,1,0:T(2,128)(2,1)}, u32[]{:S(2)}, u32[]{:S(2)}) async-start(bf16[64,2,4096]{2,1,0:T(2,128)(2,1)} %reshape.32), calls=%async_computation | async-start | bytes 2097152 | tf_op jit(solution)/shard_map/all_to_all | solution.py:202
  55.1 2.2 slice.43.refs_1_
  57.3 2.8 %collective-permute-start.9 = (bf16[64,4096]{1,0:T(8,128)(2,1)}, bf16[64,4096]{1,0:T(8,128)(2,1)}, u32[]{:S(2)}, u32[]{:S(2)}) collective-permute-start(bf16[64,4096]{1,0:T(8,128)(2,1)} %slice.43.refs_1_), channel_id=1, source_target_pairs={{0,3},{1,0},{2,1},{3,2},{4,7},{5,4},{6,5},{7,6},{8,11},{9,8},{10,9... | collective-permute-start | bytes 1572872 | tf_op jit(solution)/shard_map/ppermute | solution.py:179
  62.9 2.5 %collective-permute-start.8 = (bf16[64,4096]{1,0:T(8,128)(2,1)}, bf16[64,4096]{1,0:T(8,128)(2,1)}, u32[]{:S(2)}, u32[]{:S(2)}) collective-permute-start(bf16[64,4096]{1,0:T(8,128)(2,1)} %slice.41.refs_0_), channel_id=1, source_target_pairs={{0,3},{1,0},{2,1},{3,2},{4,7},{5,4},{6,5},{7,6},{8,11},{9,8},{10,9... | collective-permute-start | bytes 1572872 | tf_op jit(solution)/shard_map/ppermute | solution.py:179
  65.3 16.5 %all-to-all-done = bf16[64,2,4096]{2,1,0:T(2,128)(2,1)} async-done(((bf16[64,2,4096]{2,1,0:T(2,128)(2,1)}), bf16[64,2,4096]{2,1,0:T(2,128)(2,1)}, u32[]{:S(2)}, u32[]{:S(2)}) %all-to-all-start) | async-done | bytes 1048608 | tf_op jit(solution)/shard_map/all_to_all | solution.py:202
  81.9 3.2 %fusion.1 = (bf16[32,2,4096]{2,1,0:T(2,128)(2,1)}, bf16[32,2,4096]{2,1,0:T(2,128)(2,1)}) fusion(bf16[64,2,4096]{2,1,0:T(2,128)(2,1)} %all-to-all-done), kind=kLoop, calls=%fused_computation.12 | loop fusion | bytes 2097152 | tf_op jit(solution)/shard_map/slice | solution.py:177
  85.0 2.0 slice.37.refs_0_
  92.6 3.0 %collective-permute-start.11 = (bf16[64,4096]{1,0:T(8,128)(2,1)}, bf16[64,4096]{1,0:T(8,128)(2,1)}, u32[]{:S(2)}, u32[]{:S(2)}) collective-permute-start(bf16[64,4096]{1,0:T(8,128)(2,1)} %collective-permute-done.9.refs_5_), channel_id=1, source_target_pairs={{0,3},{1,0},{2,1},{3,2},{4,7},{5,4},{6,5},{7,6},{8,11},{9,8},{10,9... | collective-permute-start | bytes 1572872 | tf_op jit(solution)/shard_map/ppermute | solution.py:179
  95.6 7.9 %collective-permute-done.refs_2_ = bf16[64,4096]{1,0:T(8,128)(2,1)} collective-permute-done((bf16[64,4096]{1,0:T(8,128)(2,1)}, bf16[64,4096]{1,0:T(8,128)(2,1)}, u32[]{:S(2)}, u32[]{:S(2)}) %collective-permute-start) | collective-permute-done | bytes 524320 | tf_op jit(solution)/shard_map/ppermute | solution.py:178
  107.3 7.3 %collective-permute-done.10.refs_6_ = bf16[64,4096]{1,0:T(8,128)(2,1)S(1)} collective-permute-done((bf16[64,4096]{1,0:T(8,128)(2,1)}, bf16[64,4096]{1,0:T(8,128)(2,1)S(1)}, u32[]{:S(2)}, u32[]{:S(2)}) %collective-permute-start.10) | collective-permute-done | bytes 524320 | tf_op jit(solution)/shard_map/ppermute | solution.py:178
  121.0 5.5 %prep.1 = (bf16[4096,768]{1,0:T(8,128)(2,1)S(1)}, bf16[768,4096]{1,0:T(8,128)(2,1)S(1)}, bf16[4096,384]{1,0:T(8,128)(2,1)S(1)}) custom-call(f32[32,3]{1,0:T(8,128)S(1)} %bitcast.15, f32[32,3]{1,0:T(8,128)S(1)} %bitcast.16, f32[3,32]{1,0:T(4,128)S(1)} %bitcast.17, bf16[4096,384]{1,0:T(8,128)(2,1)S(1)} %bitcast.12, bf16[4096,384]{1,0:T(8,128)(2,1)S(1)} %bitcast.13, ...), custom_call_target="tpu_custom_call" | custom-call | flops 12582912 | bytes 25165824 | tf_op jit(solution)/shard_map/prep/pallas_call | solution.py:235
  126.5 7.7 %forward.1.refs_9_ = f32[512,768]{1,0:T(8,128)S(1)} custom-call(bf16[64,4096]{1,0:T(8,128)(2,1)S(1)} %copy-done.5, bf16[64,4096]{1,0:T(8,128)(2,1)S(1)} %copy-done.3, bf16[64,4096]{1,0:T(8,128)(2,1)} %collective-permute-done.6.refs_2_, bf16[64,4096]{1,0:T(8,128)(2,1)} %collective-permute-done.7.refs_3_, bf16[64,4096]{1,0:T(8,128)(2,1)} %collective-permute-done.8.refs_4_, ...), custom_call_target="tpu_custom_call" | custom-call | flops 3221225472 | bytes 10485760 | tf_op jit(solution)/shard_map/forward/pallas_call | solution.py:265
  137.0 7.3 %middle.1 = (bf16[512,768]{1,0:T(8,128)(2,1)S(1)}, bf16[512,128]{1,0:T(8,128)(2,1)S(1)}) custom-call(bf16[64,4096]{1,0:T(8,128)(2,1)S(1)} %copy-done.4, bf16[64,4096]{1,0:T(8,128)(2,1)S(1)} %copy-done.6, bf16[64,4096]{1,0:T(8,128)(2,1)} %collective-permute-done.refs_2_, bf16[64,4096]{1,0:T(8,128)(2,1)} %collective-permute-done.1.refs_3_, ...), custom_call_target="tpu_custom_call" | custom-call | flops 1610612736 | bytes 7340032 | tf_op jit(solution)/shard_map/middle/pallas_call | solution.py:276
  146.1 3.0 %collective-permute-start.16 = (bf16[64,2048]{1,0:T(8,128)(2,1)S(1)}, bf16[64,2048]{1,0:T(8,128)(2,1)S(1)}, u32[]{:S(2)}, u32[]{:S(2)}) collective-permute-start(bf16[64,2048]{1,0:T(8,128)(2,1)S(1)} %get-tuple-element.41), channel_id=1, source_target_pairs={{0,3},{1,0},{2,1},{3,2},{4,7},{5,4},{6,5},{7,6},{8,11},{9,8},{10,9... | collective-permute-start | bytes 786440 | tf_op jit(solution)/shard_map/ppermute | solution.py:189
  155.9 3.7 %collective-permute-start.14 = (bf16[64,2048]{1,0:T(8,128)(2,1)S(1)}, bf16[64,2048]{1,0:T(8,128)(2,1)S(1)}, u32[]{:S(2)}, u32[]{:S(2)}) collective-permute-start(bf16[64,2048]{1,0:T(8,128)(2,1)S(1)} %get-tuple-element.38), channel_id=1, source_target_pairs={{0,3},{1,0},{2,1},{3,2},{4,7},{5,4},{6,5},{7,6},{8,11},{9,8},{10,9... | collective-permute-start | bytes 786440 | tf_op jit(solution)/shard_map/ppermute | solution.py:189
  159.6 4.2 %collective-permute-done.12 = bf16[64,2048]{1,0:T(8,128)(2,1)S(1)} collective-permute-done((bf16[64,2048]{1,0:T(8,128)(2,1)S(1)}, bf16[64,2048]{1,0:T(8,128)(2,1)S(1)}, u32[]{:S(2)}, u32[]{:S(2)}) %collective-permute-start.12) | collective-permute-done | bytes 262176 | tf_op jit(solution)/shard_map/ppermute | solution.py:188
  169.2 4.2 %collective-permute-done.14 = bf16[64,2048]{1,0:T(8,128)(2,1)S(1)} collective-permute-done((bf16[64,2048]{1,0:T(8,128)(2,1)S(1)}, bf16[64,2048]{1,0:T(8,128)(2,1)S(1)}, u32[]{:S(2)}, u32[]{:S(2)}) %collective-permute-start.14) | collective-permute-done | bytes 262176 | tf_op jit(solution)/shard_map/ppermute | solution.py:189
  174.5 2.7 %collective-permute-start.23 = (bf16[64,2176]{1,0:T(8,128)(2,1)}, bf16[64,2176]{1,0:T(8,128)(2,1)S(1)}, u32[]{:S(2)}, u32[]{:S(2)}) collective-permute-start(bf16[64,2176]{1,0:T(8,128)(2,1)} %add_convert_fusion.1), channel_id=1, source_target_pairs={{0,3},{1,0},{2,1},{3,2},{4,7},{5,4},{6,5},{7,6},{8,11},{9,8},{10,9... | collective-permute-start | bytes 835592 | tf_op jit(solution)/shard_map/ppermute | solution.py:189
  181.2 7.8 %all-to-all-start.2 = ((bf16[64,2,2048]{2,1,0:T(2,128)(2,1)}), bf16[64,2,2048]{2,1,0:T(2,128)(2,1)S(1)}, u32[]{:S(2)}, u32[]{:S(2)}) async-start(bf16[64,2,2048]{2,1,0:T(2,128)(2,1)} %convert_element_type.94), calls=%async_computation.2 | async-start | bytes 1048576 | tf_op jit(solution)/shard_map/all_to_all | solution.py:202
  192.2 14.3 %all-to-all-done.2 = bf16[64,2,2048]{2,1,0:T(2,128)(2,1)S(1)} async-done(((bf16[64,2,2048]{2,1,0:T(2,128)(2,1)}), bf16[64,2,2048]{2,1,0:T(2,128)(2,1)S(1)}, u32[]{:S(2)}, u32[]{:S(2)}) %all-to-all-start.2) | async-done | bytes 524320 | tf_op jit(solution)/shard_map/all_to_all | solution.py:202
  206.6 5.9 %all-to-all-start.3 = ((bf16[64,2,2176]{2,1,0:T(2,128)(2,1)}), bf16[64,2,2176]{2,1,0:T(2,128)(2,1)S(1)}, u32[]{:S(2)}, u32[]{:S(2)}) async-start(bf16[64,2,2176]{2,1,0:T(2,128)(2,1)} %convert_element_type.107), calls=%async_computation.3 | async-start | bytes 1114112 | tf_op jit(solution)/shard_map/all_to_all | solution.py:202
  212.6 18.1 %all-to-all-done.3 = bf16[64,2,2176]{2,1,0:T(2,128)(2,1)S(1)} async-done(((bf16[64,2,2176]{2,1,0:T(2,128)(2,1)}), bf16[64,2,2176]{2,1,0:T(2,128)(2,1)S(1)}, u32[]{:S(2)}, u32[]{:S(2)}) %all-to-all-start.3) | async-done | bytes 557088 | tf_op jit(solution)/shard_map/all_to_all | solution.py:202
  (98 shorter events, 54.2 us)
Async XLA Ops:
  6.4 40.9 %all-to-all-start.1 = ((bf16[64,2,4096]{2,1,0:T(2,128)(2,1)}), bf16[64,2,4096]{2,1,0:T(2,128)(2,1)S(1)}, u32[]{:S(2)}, u32[]{:S(2)}) async-start(bf16[64,2,4096]{2,1,0:T(2,128)(2,1)} %reshape.33), calls=%async_computation.1 | async-start | bytes 2097152 | tf_op jit(solution)/shard_map/all_to_all | solution.py:202
  47.3 34.6 %all-to-all-start = ((bf16[64,2,4096]{2,1,0:T(2,128)(2,1)}), bf16[64,2,4096]{2,1,0:T(2,128)(2,1)}, u32[]{:S(2)}, u32[]{:S(2)}) async-start(bf16[64,2,4096]{2,1,0:T(2,128)(2,1)} %reshape.32), calls=%async_computation | async-start | bytes 2097152 | tf_op jit(solution)/shard_map/all_to_all | solution.py:202
  57.3 35.0 %collective-permute-start.9 = (bf16[64,4096]{1,0:T(8,128)(2,1)}, bf16[64,4096]{1,0:T(8,128)(2,1)}, u32[]{:S(2)}, u32[]{:S(2)}) collective-permute-start(bf16[64,4096]{1,0:T(8,128)(2,1)} %slice.43.refs_1_), channel_id=1, source_target_pairs={{0,3},{1,0},{2,1},{3,2},{4,7},{5,4},{6,5},{7,6},{8,11},{9,8},{10,9... | collective-permute-start | bytes 1572872 | tf_op jit(solution)/shard_map/ppermute | solution.py:179
  60.1 32.6 %collective-permute-start.7 = (bf16[64,4096]{1,0:T(8,128)(2,1)}, bf16[64,4096]{1,0:T(8,128)(2,1)}, u32[]{:S(2)}, u32[]{:S(2)}) collective-permute-start(bf16[64,4096]{1,0:T(8,128)(2,1)} %slice.43.refs_1_), channel_id=1, source_target_pairs={{0,1},{1,2},{2,3},{3,0},{4,5},{5,6},{6,7},{7,4},{8,9},{9,10},{10,1... | collective-permute-start | bytes 1572872 | tf_op jit(solution)/shard_map/ppermute | solution.py:178
  62.1 28.5 %collective-permute-start.6 = (bf16[64,4096]{1,0:T(8,128)(2,1)}, bf16[64,4096]{1,0:T(8,128)(2,1)}, u32[]{:S(2)}, u32[]{:S(2)}) collective-permute-start(bf16[64,4096]{1,0:T(8,128)(2,1)} %slice.41.refs_0_), channel_id=1, source_target_pairs={{0,1},{1,2},{2,3},{3,0},{4,5},{5,6},{6,7},{7,4},{8,9},{9,10},{10,1... | collective-permute-start | bytes 1572872 | tf_op jit(solution)/shard_map/ppermute | solution.py:178
  62.9 32.7 %collective-permute-start.8 = (bf16[64,4096]{1,0:T(8,128)(2,1)}, bf16[64,4096]{1,0:T(8,128)(2,1)}, u32[]{:S(2)}, u32[]{:S(2)}) collective-permute-start(bf16[64,4096]{1,0:T(8,128)(2,1)} %slice.41.refs_0_), channel_id=1, source_target_pairs={{0,3},{1,0},{2,1},{3,2},{4,7},{5,4},{6,5},{7,6},{8,11},{9,8},{10,9... | collective-permute-start | bytes 1572872 | tf_op jit(solution)/shard_map/ppermute | solution.py:179
  87.1 16.4 %collective-permute-start = (bf16[64,4096]{1,0:T(8,128)(2,1)}, bf16[64,4096]{1,0:T(8,128)(2,1)}, u32[]{:S(2)}, u32[]{:S(2)}) collective-permute-start(bf16[64,4096]{1,0:T(8,128)(2,1)} %slice.37.refs_0_), channel_id=1, source_target_pairs={{0,1},{1,2},{2,3},{3,0},{4,5},{5,6},{6,7},{7,4},{8,9},{9,10},{10,1... | collective-permute-start | bytes 1572872 | tf_op jit(solution)/shard_map/ppermute | solution.py:178
  90.6 15.2 %collective-permute-start.3 = (bf16[64,4096]{1,0:T(8,128)(2,1)}, bf16[64,4096]{1,0:T(8,128)(2,1)}, u32[]{:S(2)}, u32[]{:S(2)}) collective-permute-start(bf16[64,4096]{1,0:T(8,128)(2,1)} %slice.39.refs_1_), channel_id=1, source_target_pairs={{0,3},{1,0},{2,1},{3,2},{4,7},{5,4},{6,5},{7,6},{8,11},{9,8},{10,9... | collective-permute-start | bytes 1572872 | tf_op jit(solution)/shard_map/ppermute | solution.py:179
  92.3 22.2 %collective-permute-start.10 = (bf16[64,4096]{1,0:T(8,128)(2,1)}, bf16[64,4096]{1,0:T(8,128)(2,1)S(1)}, u32[]{:S(2)}, u32[]{:S(2)}) collective-permute-start(bf16[64,4096]{1,0:T(8,128)(2,1)} %collective-permute-done.6.refs_2_), channel_id=1, source_target_pairs={{0,1},{1,2},{2,3},{3,0},{4,5},{5,6},{6,7},{7,4},{8,9},{9,10},{10,1... | collective-permute-start | bytes 1572872 | tf_op jit(solution)/shard_map/ppermute | solution.py:178
  92.6 33.8 %collective-permute-start.11 = (bf16[64,4096]{1,0:T(8,128)(2,1)}, bf16[64,4096]{1,0:T(8,128)(2,1)}, u32[]{:S(2)}, u32[]{:S(2)}) collective-permute-start(bf16[64,4096]{1,0:T(8,128)(2,1)} %collective-permute-done.9.refs_5_), channel_id=1, source_target_pairs={{0,3},{1,0},{2,1},{3,2},{4,7},{5,4},{6,5},{7,6},{8,11},{9,8},{10,9... | collective-permute-start | bytes 1572872 | tf_op jit(solution)/shard_map/ppermute | solution.py:179
  95.6 38.7 %collective-permute-start.1 = (bf16[64,4096]{1,0:T(8,128)(2,1)}, bf16[64,4096]{1,0:T(8,128)(2,1)}, u32[]{:S(2)}, u32[]{:S(2)}) collective-permute-start(bf16[64,4096]{1,0:T(8,128)(2,1)} %slice.39.refs_1_), channel_id=1, source_target_pairs={{0,1},{1,2},{2,3},{3,0},{4,5},{5,6},{6,7},{7,4},{8,9},{9,10},{10,1... | collective-permute-start | bytes 1572872 | tf_op jit(solution)/shard_map/ppermute | solution.py:178
  103.5 30.8 %collective-permute-start.2 = (bf16[64,4096]{1,0:T(8,128)(2,1)}, bf16[64,4096]{1,0:T(8,128)(2,1)}, u32[]{:S(2)}, u32[]{:S(2)}) collective-permute-start(bf16[64,4096]{1,0:T(8,128)(2,1)} %slice.37.refs_0_), channel_id=1, source_target_pairs={{0,3},{1,0},{2,1},{3,2},{4,7},{5,4},{6,5},{7,6},{8,11},{9,8},{10,9... | collective-permute-start | bytes 1572872 | tf_op jit(solution)/shard_map/ppermute | solution.py:179
  105.8 29.2 %collective-permute-start.4 = (bf16[64,4096]{1,0:T(8,128)(2,1)}, bf16[64,4096]{1,0:T(8,128)(2,1)}, u32[]{:S(2)}, u32[]{:S(2)}) collective-permute-start(bf16[64,4096]{1,0:T(8,128)(2,1)} %collective-permute-done.refs_2_), channel_id=1, source_target_pairs={{0,1},{1,2},{2,3},{3,0},{4,5},{5,6},{6,7},{7,4},{8,9},{9,10},{10,1... | collective-permute-start | bytes 1572872 | tf_op jit(solution)/shard_map/ppermute | solution.py:178
  115.5 21.6 %collective-permute-start.5 = (bf16[64,4096]{1,0:T(8,128)(2,1)}, bf16[64,4096]{1,0:T(8,128)(2,1)}, u32[]{:S(2)}, u32[]{:S(2)}) collective-permute-start(bf16[64,4096]{1,0:T(8,128)(2,1)} %collective-permute-done.3.refs_5_), channel_id=1, source_target_pairs={{0,3},{1,0},{2,1},{3,2},{4,7},{5,4},{6,5},{7,6},{8,11},{9,8},{10,9... | collective-permute-start | bytes 1572872 | tf_op jit(solution)/shard_map/ppermute | solution.py:179
  150.9 14.6 %collective-permute-start.22 = (bf16[64,2176]{1,0:T(8,128)(2,1)S(1)}, bf16[64,2176]{1,0:T(8,128)(2,1)S(1)}, u32[]{:S(2)}, u32[]{:S(2)}) collective-permute-start(bf16[64,2176]{1,0:T(8,128)(2,1)S(1)} %get-tuple-element.49), channel_id=1, source_target_pairs={{0,3},{1,0},{2,1},{3,2},{4,7},{5,4},{6,5},{7,6},{8,11},{9,8},{10,9... | collective-permute-start | bytes 835592 | tf_op jit(solution)/shard_map/ppermute | solution.py:189
  151.3 16.7 %collective-permute-start.18 = (bf16[64,2176]{1,0:T(8,128)(2,1)S(1)}, bf16[64,2176]{1,0:T(8,128)(2,1)S(1)}, u32[]{:S(2)}, u32[]{:S(2)}) collective-permute-start(bf16[64,2176]{1,0:T(8,128)(2,1)S(1)} %get-tuple-element.45), channel_id=1, source_target_pairs={{0,1},{1,2},{2,3},{3,0},{4,5},{5,6},{6,7},{7,4},{8,9},{9,10},{10,1... | collective-permute-start | bytes 835592 | tf_op jit(solution)/shard_map/ppermute | solution.py:188
  153.0 36.0 %collective-permute-start.20 = (bf16[64,2176]{1,0:T(8,128)(2,1)S(1)}, bf16[64,2176]{1,0:T(8,128)(2,1)S(1)}, u32[]{:S(2)}, u32[]{:S(2)}) collective-permute-start(bf16[64,2176]{1,0:T(8,128)(2,1)S(1)} %get-tuple-element.46), channel_id=1, source_target_pairs={{0,3},{1,0},{2,1},{3,2},{4,7},{5,4},{6,5},{7,6},{8,11},{9,8},{10,9... | collective-permute-start | bytes 835592 | tf_op jit(solution)/shard_map/ppermute | solution.py:189
  155.9 17.6 %collective-permute-start.14 = (bf16[64,2048]{1,0:T(8,128)(2,1)S(1)}, bf16[64,2048]{1,0:T(8,128)(2,1)S(1)}, u32[]{:S(2)}, u32[]{:S(2)}) collective-permute-start(bf16[64,2048]{1,0:T(8,128)(2,1)S(1)} %get-tuple-element.38), channel_id=1, source_target_pairs={{0,3},{1,0},{2,1},{3,2},{4,7},{5,4},{6,5},{7,6},{8,11},{9,8},{10,9... | collective-permute-start | bytes 786440 | tf_op jit(solution)/shard_map/ppermute | solution.py:189
  165.5 13.1 %collective-permute-start.17 = (bf16[64,2048]{1,0:T(8,128)(2,1)S(1)}, bf16[64,2048]{1,0:T(8,128)(2,1)S(1)}, u32[]{:S(2)}, u32[]{:S(2)}) collective-permute-start(bf16[64,2048]{1,0:T(8,128)(2,1)S(1)} %add_convert_fusion.5), channel_id=1, source_target_pairs={{0,3},{1,0},{2,1},{3,2},{4,7},{5,4},{6,5},{7,6},{8,11},{9,8},{10,9... | collective-permute-start | bytes 786440 | tf_op jit(solution)/shard_map/ppermute | solution.py:189
  168.0 11.8 %collective-permute-start.13 = (bf16[64,2048]{1,0:T(8,128)(2,1)S(1)}, bf16[64,2048]{1,0:T(8,128)(2,1)S(1)}, u32[]{:S(2)}, u32[]{:S(2)}) collective-permute-start(bf16[64,2048]{1,0:T(8,128)(2,1)S(1)} %add_convert_fusion.7), channel_id=1, source_target_pairs={{0,1},{1,2},{2,3},{3,0},{4,5},{5,6},{6,7},{7,4},{8,9},{9,10},{10,1... | collective-permute-start | bytes 786440 | tf_op jit(solution)/shard_map/ppermute | solution.py:188
  173.4 15.6 %collective-permute-start.21 = (bf16[64,2176]{1,0:T(8,128)(2,1)S(1)}, bf16[64,2176]{1,0:T(8,128)(2,1)S(1)}, u32[]{:S(2)}, u32[]{:S(2)}) collective-permute-start(bf16[64,2176]{1,0:T(8,128)(2,1)S(1)} %get-tuple-element.47), channel_id=1, source_target_pairs={{0,1},{1,2},{2,3},{3,0},{4,5},{5,6},{6,7},{7,4},{8,9},{9,10},{10,1... | collective-permute-start | bytes 835592 | tf_op jit(solution)/shard_map/ppermute | solution.py:188
  174.5 14.5 %collective-permute-start.23 = (bf16[64,2176]{1,0:T(8,128)(2,1)}, bf16[64,2176]{1,0:T(8,128)(2,1)S(1)}, u32[]{:S(2)}, u32[]{:S(2)}) collective-permute-start(bf16[64,2176]{1,0:T(8,128)(2,1)} %add_convert_fusion.1), channel_id=1, source_target_pairs={{0,3},{1,0},{2,1},{3,2},{4,7},{5,4},{6,5},{7,6},{8,11},{9,8},{10,9... | collective-permute-start | bytes 835592 | tf_op jit(solution)/shard_map/ppermute | solution.py:189
  181.2 25.3 %all-to-all-start.2 = ((bf16[64,2,2048]{2,1,0:T(2,128)(2,1)}), bf16[64,2,2048]{2,1,0:T(2,128)(2,1)S(1)}, u32[]{:S(2)}, u32[]{:S(2)}) async-start(bf16[64,2,2048]{2,1,0:T(2,128)(2,1)} %convert_element_type.94), calls=%async_computation.2 | async-start | bytes 1048576 | tf_op jit(solution)/shard_map/all_to_all | solution.py:202
  206.6 24.1 %all-to-all-start.3 = ((bf16[64,2,2176]{2,1,0:T(2,128)(2,1)}), bf16[64,2,2176]{2,1,0:T(2,128)(2,1)S(1)}, u32[]{:S(2)}, u32[]{:S(2)}) async-start(bf16[64,2,2176]{2,1,0:T(2,128)(2,1)} %convert_element_type.107), calls=%async_computation.3 | async-start | bytes 1114112 | tf_op jit(solution)/shard_map/all_to_all | solution.py:202
  (22 other events, 335.0 us)

commit v2 on v1

v2 whole, which is shorter than its diff:
```python
import functools

import jax
import jax.numpy as jnp
from jax import lax
from jax.experimental import pallas as pl
from jax.experimental.pallas import tpu as pltpu
from jax.sharding import PartitionSpec as P

BF = jnp.bfloat16
F32 = jnp.float32
BLOCK = 128
VMEM_MIB = 56
SPAN = 2048
MIB = 1 << 20
VMEM = pl.BlockSpec(memory_space=pltpu.VMEM)
SMEM = pl.BlockSpec(memory_space=pltpu.SMEM)


def params(mib):
    return pltpu.CompilerParams(vmem_limit_bytes=mib * MIB)


def cost(flops, moved):
    return pl.CostEstimate(flops=flops, bytes_accessed=moved, transcendentals=0)


def dot(a, b, dims=((1,), (0,))):
    return lax.dot_general(a, b, (dims, ((), ())), preferred_element_type=F32)


def pack_kernel(rows, t_ref, ids_ref, gates_ref, x_ref, d_ref, sa_ref, comb_ref, pick_ref, place_ref):
    t = t_ref[0]
    top, group = ids_ref.shape
    experts = sa_ref.shape[0]
    slots = 2 * experts
    width = x_ref.shape[1]
    quarters = group // rows
    lane = lax.broadcasted_iota(jnp.int32, (slots, group), 0)
    expert, copy = lane % experts, lane // experts
    hits = [ids_ref[k : k + 1, :] == expert for k in range(top)]
    member = functools.reduce(jnp.logical_or, hits)
    member = jnp.where(member, 1.0, 0.0).astype(BF)
    first = lax.broadcasted_iota(jnp.int32, (group, group), 0)
    later = lax.broadcasted_iota(jnp.int32, (group, group), 1)
    before = (first < later) & (first // rows == later // rows)
    prior = dot(member, jnp.where(before, 1.0, 0.0).astype(BF))
    ranked = prior == copy.astype(F32)

    def keep(quarter):
        at = lax.broadcasted_iota(jnp.int32, (group, rows), 0)
        own = quarter * rows + lax.broadcasted_iota(jnp.int32, (group, rows), 1)
        return jnp.where(at == own, 1.0, 0.0).astype(BF)

    mine = keep(t)
    weight = jnp.zeros((slots, group), F32)
    every = jnp.zeros((slots, group), F32)
    for k in range(top):
        hit = jnp.where(hits[k] & ranked, 1.0, 0.0)
        weight = weight + hit * gates_ref[k : k + 1, :].astype(F32)
        pick_ref[k] = dot(hit.astype(BF), mine).astype(BF)
        every = every + hit
    comb_ref[...] = dot(mine, weight.astype(BF), ((0,), (1,))).astype(BF)
    every = every.astype(BF)
    for q, off in enumerate((0, quarters - 1, 1, quarters // 2)):
        place_ref[q] = dot(every[experts:], keep(lax.rem(t + off, quarters))).astype(BF)
    send = dot(every, mine).astype(BF)
    step = 1024
    for c in range(0, width, step):
        moved = dot(send, x_ref[:, c : c + step]).astype(BF)
        sa_ref[:, c : c + step] = moved[:experts]
        sa_ref[:, 2 * width + c : 2 * width + c + step] = moved[experts:]
        sa_ref[:, width + c : width + c + step] = dot(send[:experts], d_ref[:, c : c + step]).astype(BF)


def place_kernel(place_ref, *refs):
    pieces, out_ref = refs[:-1], refs[-1]
    width = pieces[0].shape[1]
    step = 1024
    for q, piece in enumerate(pieces):
        for c in range(0, width, step):
            moved = dot(place_ref[q], piece[:, c : c + step]).astype(BF)
            out_ref[:, q * width + c : q * width + c + step] = moved


def prep_kernel(sg_ref, su_ref, sd_ref, wg_ref, wu_ref, wd_ref, both_ref, back_ref, down_ref):
    i = pl.program_id(0)
    depth, hid = wg_ref.shape
    for b in range(depth // BLOCK):
        at = i * (depth // BLOCK) + b
        rs = slice(b * BLOCK, (b + 1) * BLOCK)
        for j in range(hid // BLOCK):
            cs = slice(j * BLOCK, (j + 1) * BLOCK)
            ct = slice(hid + j * BLOCK, hid + (j + 1) * BLOCK)
            g = wg_ref[rs, cs].astype(F32) * sg_ref[at, j]
            u = wu_ref[rs, cs].astype(F32) * su_ref[at, j]
            d = wd_ref[cs, rs].astype(F32) * sd_ref[j, at]
            both_ref[rs, cs] = g.astype(BF)
            both_ref[rs, ct] = u.astype(BF)
            back_ref[cs, rs] = g.T.astype(BF)
            back_ref[ct, rs] = u.T.astype(BF)
            down_ref[rs, cs] = d.T.astype(BF)


def joined(refs):
    return jnp.concatenate([r[...] for r in refs], axis=0)


def expert_kernel(pieces, steps, d_pieces, *refs):
    x_refs, refs = refs[:pieces], refs[pieces:]
    d_refs, refs = refs[:d_pieces], refs[d_pieces:]
    both_ref, down_ref, back_ref = refs[:3]
    outs = refs[3:-4]
    pre_ref, raw_ref, made_ref, gate_ref = refs[-4:]
    i = pl.program_id(0)
    hid = raw_ref.shape[1]

    @pl.when(i < steps)
    def _():
        pre = dot(joined(x_refs), both_ref[...])
        raw = dot(joined(d_refs), down_ref[...])

        @pl.when(i == 0)
        def _():
            pre_ref[...] = pre
            raw_ref[...] = raw

        @pl.when(i > 0)
        def _():
            pre_ref[...] += pre
            raw_ref[...] += raw

    @pl.when(i == steps)
    def _():
        step = 64
        for r in range(0, raw_ref.shape[0], step):
            rs = slice(r, r + step)
            raw = raw_ref[rs, :]
            pre = pre_ref[rs, :hid]
            up = pre_ref[rs, hid:]
            sig = 1.0 / (1.0 + jnp.exp(-pre))
            act = pre * sig
            total = jnp.sum(act * up * raw, axis=1, keepdims=True)
            made_ref[rs, hid:] = (raw * act).astype(BF)
            made_ref[rs, :hid] = (raw * up * sig * (1.0 + pre * (1.0 - sig))).astype(BF)
            col = lax.broadcasted_iota(jnp.int32, (step, BLOCK), 1)
            gate_ref[rs, :] = jnp.where(col == 0, total, 0.0).astype(BF)

    @pl.when(i >= steps)
    def _():
        def put(cs, value):
            at = 0
            for o in outs:
                o[:, cs] = value[at : at + o.shape[0]]
                at += o.shape[0]

        width = back_ref.shape[1]
        step = 512
        for c in range(0, width, step):
            cs = slice(c, c + step)
            put(cs, dot(made_ref[...], back_ref[:, cs]).astype(BF))
        put(slice(width, width + BLOCK), gate_ref[...])


def combine_kernel(comb_ref, pick_ref, a_ref, b_ref, tok_ref, gate_ref):
    experts = a_ref.shape[0]
    comb = comb_ref[...]
    half = tok_ref.shape[1] // 2
    step = 1024
    for h in range(2):
        for c in range(0, half, step):
            cs = slice(h * (half + BLOCK) + c, h * (half + BLOCK) + c + step)
            back = jnp.concatenate([a_ref[:, cs], b_ref[:, cs]], axis=0)
            tok_ref[:, h * half + c : h * half + c + step] = dot(comb, back).astype(BF)
    sums = jnp.concatenate([a_ref[:, half : half + BLOCK], b_ref[:, half : half + BLOCK]], axis=0)
    for k in range(pick_ref.shape[0]):
        gate_ref[k : k + 1, :] = dot(sums, pick_ref[k], ((0,), (0,)))[:1, :]


def ring(n, by):
    return [(i, (i + by) % n) for i in range(n)]


def to_right(v, n):
    return lax.ppermute(v, "tp", ring(n, 1))


def to_left(v, n):
    return lax.ppermute(v, "tp", ring(n, -1))


def across(v, n):
    return lax.ppermute(v, "tp", ring(n, n // 2))


def gather(x, n, direct):
    left, right = to_right(x, n), to_left(x, n)
    if direct:
        return [x, left, right, across(x, n)]
    h = x.shape[0] // 2
    return [x, left, right, to_right(left[:h], n), to_left(right[h:], n)]


def home(terms, n):
    return home_sum(home_sends(terms, n))


def home_sends(terms, n):
    own, left, right, opposite = terms
    return [own, to_left(left, n), to_right(right, n), across(opposite, n)]


def home_sum(parts):
    return sum(p.astype(F32) for p in parts).astype(BF)


def exchange(x):
    rows, width = x.shape
    y = lax.all_to_all(x.reshape(rows, 2, width // 2), "ep", split_axis=0, concat_axis=0, tiled=True)
    return y.reshape(rows, width)


def shards(tokens, grad_out, expert_ids, gate_weights, w_gate, w_up, w_down, scale_gate, scale_up, scale_down):
    n_tp = lax.axis_size("tp")
    experts = lax.axis_size("ep")
    rows, width = tokens.shape
    top = expert_ids.shape[1]
    hid = w_gate.shape[2]
    slots = 2 * experts
    t = lax.axis_index("tp").astype(jnp.int32).reshape(1)

    send_a, comb, pick, place = pl.pallas_call(
        functools.partial(pack_kernel, rows),
        in_specs=[SMEM, VMEM, VMEM, VMEM, VMEM],
        out_specs=[VMEM] * 4,
        out_shape=[
            jax.ShapeDtypeStruct((experts, 3 * width), BF),
            jax.ShapeDtypeStruct((rows, slots), BF),
            jax.ShapeDtypeStruct((top, slots, rows), BF),
            jax.ShapeDtypeStruct((n_tp, experts, rows), BF),
        ],
        compiler_params=params(58),
        cost_estimate=cost(4 * slots * rows * width, 6 * slots * width),
        name="pack",
    )(t, expert_ids.T, gate_weights.T, tokens, grad_out)

    send_d = pl.pallas_call(
        place_kernel,
        in_specs=[VMEM] * (1 + n_tp),
        out_specs=VMEM,
        out_shape=jax.ShapeDtypeStruct((experts, n_tp * width), BF),
        compiler_params=params(58),
        cost_estimate=cost(2 * n_tp * experts * rows * width, 3 * n_tp * experts * width),
        name="place",
    )(place, *gather(grad_out, n_tp, True))

    depth = 512
    steps = width // depth
    both, back, down = pl.pallas_call(
        prep_kernel,
        grid=(steps,),
        in_specs=[
            SMEM,
            SMEM,
            SMEM,
            pl.BlockSpec((depth, hid), lambda i: (i, 0)),
            pl.BlockSpec((depth, hid), lambda i: (i, 0)),
            pl.BlockSpec((hid, depth), lambda i: (0, i)),
        ],
        out_specs=[
            pl.BlockSpec((depth, 2 * hid), lambda i: (i, 0)),
            pl.BlockSpec((2 * hid, depth), lambda i: (0, i)),
            pl.BlockSpec((depth, hid), lambda i: (i, 0)),
        ],
        out_shape=[
            jax.ShapeDtypeStruct((width, 2 * hid), BF),
            jax.ShapeDtypeStruct((2 * hid, width), BF),
            jax.ShapeDtypeStruct((width, hid), BF),
        ],
        compiler_params=params(58),
        cost_estimate=cost(8 * width * hid, 16 * width * hid),
        name="prep",
    )(scale_gate[0], scale_up[0], scale_down[0], w_gate[0], w_up[0], w_down[0])

    count = n_tp * experts
    span = SPAN
    turns = width // span
    last = turns - 1

    def products(x_pieces, d_pieces, heights):
        pieces = list(x_pieces) + list(d_pieces)

        def spec(piece):
            array, column = piece
            return pl.BlockSpec(
                (array.shape[0], span), lambda i: (0, column // span + jnp.minimum(i, last))
            )

        return pl.pallas_call(
            functools.partial(expert_kernel, len(x_pieces), turns, len(d_pieces)),
            grid=(turns + 2,),
            in_specs=[spec(p) for p in pieces]
            + [
                pl.BlockSpec((span, 2 * hid), lambda i: (jnp.minimum(i, last), 0)),
                pl.BlockSpec((span, hid), lambda i: (jnp.minimum(i, last), 0)),
                pl.BlockSpec((2 * hid, width // 2), lambda i: (0, jnp.maximum(i - turns, 0))),
            ],
            out_specs=[
                pl.BlockSpec((h, width // 2 + BLOCK), lambda i: (0, jnp.maximum(i - turns, 0)))
                for h in heights
            ],
            out_shape=[jax.ShapeDtypeStruct((h, width + 2 * BLOCK), BF) for h in heights],
            scratch_shapes=[
                pltpu.VMEM((count, 2 * hid), F32),
                pltpu.VMEM((count, hid), F32),
                pltpu.VMEM((count, 2 * hid), BF),
                pltpu.VMEM((count, BLOCK), BF),
            ],
            compiler_params=params(VMEM_MIB),
            cost_estimate=cost(10 * count * width * hid, 10 * width * hid + 6 * count * width),
            name="products",
        )(*[array for array, _ in pieces], both, down, back)

    send_d = send_d.reshape(experts, n_tp, width)
    rows_in, send_d, both, back, down = lax.optimization_barrier(
        (exchange(send_a), send_d, both, back, down)
    )
    pieces_a = gather(rows_in[:, : 2 * width], n_tp, False)
    rows_b, *pieces_a[3:] = lax.optimization_barrier((rows_in[:, 2 * width :], *pieces_a[3:]))
    pieces_b = gather(rows_b, n_tp, True)
    rows_d = lax.all_to_all(send_d, "ep", split_axis=0, concat_axis=0, tiled=True)
    rows_d = rows_d.reshape(experts, n_tp * width)
    terms_a = products(
        [(p, 0) for p in pieces_a], [(p, width) for p in pieces_a], [experts] * n_tp
    )
    sent_a = home_sends(terms_a, n_tp)
    first, *pieces_b, rows_d = lax.optimization_barrier((terms_a[0], *pieces_b, rows_d))
    terms_b = products(
        [(p, 0) for p in pieces_b], [(rows_d, q * width) for q in range(n_tp)], [experts] * n_tp
    )
    home_a = home_sum([first, *sent_a[1:]])
    home_a, *terms_b = lax.optimization_barrier((home_a, *terms_b))
    home_b = home(terms_b, n_tp)
    back_a, back_b = exchange(home_a), exchange(home_b)

    grad_rows, grad_gates = pl.pallas_call(
        combine_kernel,
        in_specs=[VMEM] * 4,
        out_specs=[VMEM, VMEM],
        out_shape=[
            jax.ShapeDtypeStruct((rows, width), BF),
            jax.ShapeDtypeStruct((top, rows), F32),
        ],
        compiler_params=params(VMEM_MIB),
        cost_estimate=cost(2 * slots * rows * width, 3 * slots * width),
        name="combine",
    )(comb, pick, back_a, back_b)
    return grad_rows, grad_gates.T


def solution(mesh):
    return jax.shard_map(
        shards,
        mesh=mesh,
        in_specs=(
            P(("ep", "tp"), None),
            P(("ep", "tp"), None),
            P("ep", None),
            P("ep", None),
            P("ep", None, "tp"),
            P("ep", None, "tp"),
            P("ep", "tp", None),
            P("ep", None, "tp"),
            P("ep", None, "tp"),
            P("ep", "tp", None),
        ),
        out_specs=(P(("ep", "tp"), None), P(("ep", "tp"), None)),
        check_vma=False,
    )
```

time: 234 us -> 225 us (0.962)
  Pallas kernels: 26 us -> 43.6 us
  starting transfers between devices: 68 us -> 55.9 us
  waiting for transfers between devices: 106 us -> 97 us
  local copies, waits for them, and re-layouts: 27.9 us -> 23.4 us
    all_to_all x4, waiting for transfers between devices: 76.2 us -> 35.1 us  [the longest x3 35.1 us: exchange(): lax.all_to_all(x.reshape(rows, 2, width // 2), 'ep', split_axis=0, concat...]
    ppermute x24 -> x16, waiting for transfers between devices: 29.6 us -> 61.9 us  [the longest x6 36.8 us: to_left(): return lax.ppermute(v, 'tp', ring(n, -1))]
    ppermute x24 -> x16, starting transfers between devices: 36.4 us -> 22 us  [the longest x6 14.6 us: to_left(): return lax.ppermute(v, 'tp', ring(n, -1))]
    slice x6 -> x4, local copies, waits for them, and re-layouts: 13.4 us -> 2.5 us  [the longest x1 1.29 us: shards(): pieces_a = gather(rows_in[:, :2 * width], n_tp, False)]
    pallas_call x5 -> x4, Pallas kernels: 19.6 us -> 28.7 us  [the longest x2 23.1 us: products(): pl.pallas_call(functools.partial(expert_kernel, len(x_pieces), turns, len...]
    reshape x4, local copies, waits for them, and re-layouts: 3.42 us -> 11.3 us  [the longest x3 6.76 us: exchange(): x.reshape(rows, 2, width // 2)]
    pallas_call x1, Pallas kernels: 5.47 us -> 11.8 us  [shards(): pl.pallas_call(prep_kernel, grid=(steps,), in_specs=[SMEM, SMEM, SMEM, pl...]
    unnamed x37 -> x39, local copies, waits for them, and re-layouts: 8.7 us -> 8.26 us
  transfers between devices with their start and end apart: 28 -> 20, of which waited for: 14 -> 12; matrix products, arithmetic and copies ran while one was open for 9% -> 7% of each run, Pallas kernels for 6% -> 17%
where the time goes in v2:
time: 225 us; the launch traced here: 223 us
  waiting for transfers between devices  97 us (43%)
  starting transfers between devices  55.9 us (25%)
  Pallas kernels  43.6 us (19%)
  local copies, waits for them, and re-layouts  23.4 us (10%)
    ppermute x6, waiting for transfers between devices, to_left(): return lax.ppermute(v, 'tp', ring(n, -1))  36.8 us
    all_to_all x3, waiting for transfers between devices, exchange(): lax.all_to_all(x.reshape(rows, 2, width // 2), 'ep', split_axis=0, concat...  35.1 us
    all_to_all x3, starting transfers between devices, exchange(): lax.all_to_all(x.reshape(rows, 2, width // 2), 'ep', split_axis=0, concat...  28.4 us
    pallas_call x2, Pallas kernels, products(): pl.pallas_call(functools.partial(expert_kernel, len(x_pieces), turns, len...  23.1 us
    ppermute x6, waiting for transfers between devices, to_right(): return lax.ppermute(v, 'tp', ring(n, 1))  16 us
    ppermute x6, starting transfers between devices, to_left(): return lax.ppermute(v, 'tp', ring(n, -1))  14.6 us
    pallas_call x1, Pallas kernels, shards(): pl.pallas_call(prep_kernel, grid=(steps,), in_specs=[SMEM, SMEM, SMEM, pl...  11.8 us
    ppermute x4, waiting for transfers between devices, across(): return lax.ppermute(v, 'tp', ring(n, n // 2))  9.14 us
  transfers between devices with their start and end apart: 20, of which 12 were waited for; matrix products, arithmetic and copies ran while one was open for 7% of the time, Pallas kernels for 17%

profile of v2, /device:TPU:8, one launch (start us, length us, event | category | flops | bytes accessed | tf_op | source)
XLA Modules:
  0.0 222.5 jit_solution(16180796874516164941)
XLA Ops:
  0.6 3.2 %pack.1 = (bf16[64,12288]{1,0:T(8,128)(2,1)}, bf16[32,128]{1,0:T(8,128)(2,1)}, bf16[3,128,32]{2,1,0:T(8,128)(2,1)}, bf16[4,64,32]{2,1,0:T(8,128)(2,1)}) custom-call(s32[1]{0:T(128)} %bitcast.t_ref, s32[3,128]{1,0:T(4,128)} %bitcast.38, bf16[3,128]{1,0:T(4,128)(2,1)} %bitcast.39, bf16[32,4096]{1,0:T(8,128)(2,1)} %x_ref.1, bf16[32,4096]{1,0:T(8,128)(2,1)} %refs_0_.1), custom_call_target="tpu_custom_call" | custom-call | flops 67108864 | bytes 3145728 | tf_op jit(solution)/shard_map/pack/pallas_call | solution.py:232
  3.8 4.9 %reshape.32 = bf16[64,2,6144]{2,1,0:T(2,128)(2,1)} reshape(bf16[64,12288]{1,0:T(8,128)(2,1)} %get-tuple-element.40) | data formatting | bytes 3145728 | tf_op jit(solution)/shard_map/reshape | solution.py:219
  8.7 12.2 %all-to-all-start = ((bf16[64,2,6144]{2,1,0:T(2,128)(2,1)}), bf16[64,2,6144]{2,1,0:T(2,128)(2,1)S(1)}, u32[]{:S(2)}, u32[]{:S(2)}) async-start(bf16[64,2,6144]{2,1,0:T(2,128)(2,1)} %reshape.32), calls=%async_computation | async-start | bytes 3145728 | tf_op jit(solution)/shard_map/all_to_all | solution.py:219
  20.9 2.8 %collective-permute-start.1 = (bf16[32,4096]{1,0:T(8,128)(2,1)S(1)}, bf16[32,4096]{1,0:T(8,128)(2,1)S(1)}, u32[]{:S(2)}, u32[]{:S(2)}) collective-permute-start(bf16[32,4096]{1,0:T(8,128)(2,1)S(1)} %copy-done.6), channel_id=1, source_target_pairs={{0,3},{1,0},{2,1},{3,2},{4,7},{5,4},{6,5},{7,6},{8,11},{9,8},{10,9... | collective-permute-start | bytes 786440 | tf_op jit(solution)/shard_map/ppermute | solution.py:189
  28.0 11.8 %prep.1 = (bf16[4096,768]{1,0:T(8,128)(2,1)}, bf16[768,4096]{1,0:T(8,128)(2,1)}, bf16[4096,384]{1,0:T(8,128)(2,1)}) custom-call(f32[32,3]{1,0:T(8,128)} %bitcast.35, f32[32,3]{1,0:T(8,128)} %bitcast.36, f32[3,32]{1,0:T(4,128)} %bitcast.37, bf16[4096,384]{1,0:T(8,128)(2,1)} %bitcast.28, bf16[4096,384]{1,0:T(8,128)(2,1)} %bitcast.29, bf16[384,4096]{1,0:T(8,128)(2,1)} %bitcast.30), custom_call_target="tpu_custom_call" | custom-call | flops 12582912 | bytes 25165824 | tf_op jit(solution)/shard_map/prep/pallas_call | solution.py:259
  40.7 3.2 %place.1 = bf16[64,16384]{1,0:T(8,128)(2,1)} custom-call(bf16[4,64,32]{2,1,0:T(8,128)(2,1)} %get-tuple-element.41.place_ref, bf16[32,4096]{1,0:T(8,128)(2,1)} %refs_0_.1, bf16[32,4096]{1,0:T(8,128)(2,1)} %copy-done.11, bf16[32,4096]{1,0:T(8,128)(2,1)} %copy-done.10, bf16[32,4096]{1,0:T(8,128)(2,1)} %copy-done.12), custom_call_target="tpu_custom_call" | custom-call | flops 67108864 | bytes 3145728 | tf_op jit(solution)/shard_map/place/pallas_call | solution.py:247
  43.9 4.5 %reshape.34 = bf16[64,4,4096]{2,1,0:T(4,128)(2,1)} reshape(bf16[64,16384]{1,0:T(8,128)(2,1)} %place.1) | data formatting | bytes 4194304 | tf_op jit(solution)/shard_map/reshape | solution.py:324
  48.4 12.5 %all-to-all-done = bf16[64,2,6144]{2,1,0:T(2,128)(2,1)S(1)} async-done(((bf16[64,2,6144]{2,1,0:T(2,128)(2,1)}), bf16[64,2,6144]{2,1,0:T(2,128)(2,1)S(1)}, u32[]{:S(2)}, u32[]{:S(2)}) %all-to-all-start) | async-done | bytes 1572896 | tf_op jit(solution)/shard_map/all_to_all | solution.py:219
  62.6 5.4 %all-to-all-start.1 = ((bf16[64,4,4096]{2,1,0:T(4,128)(2,1)}), bf16[64,4,4096]{2,1,0:T(4,128)(2,1)S(1)}, u32[]{:S(2)}, u32[]{:S(2)}) async-start(bf16[64,4,4096]{2,1,0:T(4,128)(2,1)} %reshape.34), calls=%async_computation.1 | async-start | bytes 4194304 | tf_op jit(solution)/shard_map/all_to_all | solution.py:331
  69.4 2.8 %collective-permute-start.4 = (bf16[64,8192]{1,0:T(8,128)(2,1)S(1)}, bf16[64,8192]{1,0:T(8,128)(2,1)S(1)}, u32[]{:S(2)}, u32[]{:S(2)}) collective-permute-start(bf16[64,8192]{1,0:T(8,128)(2,1)S(1)} %slice.12.refs_0_.refs_5_), channel_id=1, source_target_pairs={{0,3},{1,0},{2,1},{3,2},{4,7},{5,4},{6,5},{7,6},{8,11},{9,8},{10,9... | collective-permute-start | bytes 3145736 | tf_op jit(solution)/shard_map/ppermute | solution.py:189
  72.2 22.7 %collective-permute-done.4.refs_2_.refs_7_ = bf16[64,8192]{1,0:T(8,128)(2,1)S(1)} collective-permute-done((bf16[64,8192]{1,0:T(8,128)(2,1)S(1)}, bf16[64,8192]{1,0:T(8,128)(2,1)S(1)}, u32[]{:S(2)}, u32[]{:S(2)}) %collective-permute-start.4) | collective-permute-done | bytes 1048608 | tf_op jit(solution)/shard_map/ppermute | solution.py:189
  95.0 3.8 %collective-permute-start.6 = (bf16[32,8192]{1,0:T(8,128)(2,1)S(1)}, bf16[32,8192]{1,0:T(8,128)(2,1)S(1)}, u32[]{:S(2)}, u32[]{:S(2)}) collective-permute-start(bf16[32,8192]{1,0:T(8,128)(2,1)S(1)} %slice.17), channel_id=1, source_target_pairs={{0,3},{1,0},{2,1},{3,2},{4,7},{5,4},{6,5},{7,6},{8,11},{9,8},{10,9... | collective-permute-start | bytes 1572872 | tf_op jit(solution)/shard_map/ppermute | solution.py:189
  100.2 9.2 %collective-permute-done.6.refs_4_.refs_9_ = bf16[32,8192]{1,0:T(8,128)(2,1)S(1)} collective-permute-done((bf16[32,8192]{1,0:T(8,128)(2,1)S(1)}, bf16[32,8192]{1,0:T(8,128)(2,1)S(1)}, u32[]{:S(2)}, u32[]{:S(2)}) %collective-permute-start.6) | collective-permute-done | bytes 524320 | tf_op jit(solution)/shard_map/ppermute | solution.py:189
  109.4 3.7 %collective-permute-done.5.refs_3_.refs_8_ = bf16[32,8192]{1,0:T(8,128)(2,1)S(1)} collective-permute-done((bf16[32,8192]{1,0:T(8,128)(2,1)S(1)}, bf16[32,8192]{1,0:T(8,128)(2,1)S(1)}, u32[]{:S(2)}, u32[]{:S(2)}) %collective-permute-start.5) | collective-permute-done | bytes 524320 | tf_op jit(solution)/shard_map/ppermute | solution.py:185
  115.2 11.6 %products.2 = (bf16[64,4352]{1,0:T(8,128)(2,1)}, bf16[64,4352]{1,0:T(8,128)(2,1)}, bf16[64,4352]{1,0:T(8,128)(2,1)}, bf16[64,4352]{1,0:T(8,128)(2,1)}) custom-call(bf16[64,8192]{1,0:T(8,128)(2,1)} %copy-done, bf16[64,8192]{1,0:T(8,128)(2,1)} %copy-done.2, bf16[64,8192]{1,0:T(8,128)(2,1)} %copy-done.1, bf16[32,8192]{1,0:T(8,128)(2,1)} %copy-done.4, ...), custom_call_target="tpu_custom_call" | custom-call | flops 4026531840 | bytes 22020096 | tf_op jit(solution)/shard_map/products/pallas_call | solution.py:299
  126.7 3.0 %collective-permute-start.10 = (bf16[64,4352]{1,0:T(8,128)(2,1)}, bf16[64,4352]{1,0:T(8,128)(2,1)S(1)}, u32[]{:S(2)}, u32[]{:S(2)}) collective-permute-start(bf16[64,4352]{1,0:T(8,128)(2,1)} %get-tuple-element.55), channel_id=1, source_target_pairs={{0,3},{1,0},{2,1},{3,2},{4,7},{5,4},{6,5},{7,6},{8,11},{9,8},{10,9... | collective-permute-start | bytes 1671176 | tf_op jit(solution)/shard_map/ppermute | solution.py:189
  133.2 2.6 %copy.18 = bf16[8,8,4,4096]{3,1,2,0:T(8,128)(2,1)} copy(bf16[8,8,4,4096]{3,2,1,0:T(4,128)(2,1)S(1)} %bitcast.24) | data formatting | bytes 4194304
  138.3 11.6 %products.3 = (bf16[64,4352]{1,0:T(8,128)(2,1)}, bf16[64,4352]{1,0:T(8,128)(2,1)}, bf16[64,4352]{1,0:T(8,128)(2,1)}, bf16[64,4352]{1,0:T(8,128)(2,1)}) custom-call(bf16[64,4096]{1,0:T(8,128)(2,1)} %copy-done.5, bf16[64,4096]{1,0:T(8,128)(2,1)} %collective-permute-done.7.refs_1_, bf16[64,4096]{1,0:T(8,128)(2,1)} %collective-permute-done.8.refs_2_, ...), custom_call_target="tpu_custom_call" | custom-call | flops 4026531840 | bytes 22020096 | tf_op jit(solution)/shard_map/products/pallas_call | solution.py:299
  152.7 9.1 %collective-permute-done.12 = bf16[64,4352]{1,0:T(8,128)(2,1)} collective-permute-done((bf16[64,4352]{1,0:T(8,128)(2,1)}, bf16[64,4352]{1,0:T(8,128)(2,1)}, u32[]{:S(2)}, u32[]{:S(2)}) %collective-permute-start.12) | collective-permute-done | bytes 557088 | tf_op jit(solution)/shard_map/ppermute | solution.py:193
  166.7 10.3 %all-to-all-start.2 = ((bf16[64,2,2176]{2,1,0:T(2,128)(2,1)}), bf16[64,2,2176]{2,1,0:T(2,128)(2,1)S(1)}, u32[]{:S(2)}, u32[]{:S(2)}) async-start(bf16[64,2,2176]{2,1,0:T(2,128)(2,1)} %reshape.36), calls=%async_computation.2 | async-start | bytes 1114112 | tf_op jit(solution)/shard_map/all_to_all | solution.py:219
  179.2 9.7 %collective-permute-done.14 = bf16[64,4352]{1,0:T(8,128)(2,1)S(1)} collective-permute-done((bf16[64,4352]{1,0:T(8,128)(2,1)}, bf16[64,4352]{1,0:T(8,128)(2,1)S(1)}, u32[]{:S(2)}, u32[]{:S(2)}) %collective-permute-start.14) | collective-permute-done | bytes 557088 | tf_op jit(solution)/shard_map/ppermute | solution.py:185
  190.1 5.2 %all-to-all-done.2 = bf16[64,2,2176]{2,1,0:T(2,128)(2,1)S(1)} async-done(((bf16[64,2,2176]{2,1,0:T(2,128)(2,1)}), bf16[64,2,2176]{2,1,0:T(2,128)(2,1)S(1)}, u32[]{:S(2)}, u32[]{:S(2)}) %all-to-all-start.2) | async-done | bytes 557088 | tf_op jit(solution)/shard_map/all_to_all | solution.py:219
  195.2 5.9 %all-to-all-start.3 = ((bf16[64,2,2176]{2,1,0:T(2,128)(2,1)}), bf16[64,2,2176]{2,1,0:T(2,128)(2,1)S(1)}, u32[]{:S(2)}, u32[]{:S(2)}) async-start(bf16[64,2,2176]{2,1,0:T(2,128)(2,1)} %reshape.38), calls=%async_computation.3 | async-start | bytes 1114112 | tf_op jit(solution)/shard_map/all_to_all | solution.py:219
  202.0 17.4 %all-to-all-done.3 = bf16[64,2,2176]{2,1,0:T(2,128)(2,1)S(1)} async-done(((bf16[64,2,2176]{2,1,0:T(2,128)(2,1)}), bf16[64,2,2176]{2,1,0:T(2,128)(2,1)S(1)}, u32[]{:S(2)}, u32[]{:S(2)}) %all-to-all-start.3) | async-done | bytes 557088 | tf_op jit(solution)/shard_map/all_to_all | solution.py:219
  (73 shorter events, 32.5 us)
Async XLA Ops:
  8.7 52.3 %all-to-all-start = ((bf16[64,2,6144]{2,1,0:T(2,128)(2,1)}), bf16[64,2,6144]{2,1,0:T(2,128)(2,1)S(1)}, u32[]{:S(2)}, u32[]{:S(2)}) async-start(bf16[64,2,6144]{2,1,0:T(2,128)(2,1)} %reshape.32), calls=%async_computation | async-start | bytes 3145728 | tf_op jit(solution)/shard_map/all_to_all | solution.py:219
  20.9 18.9 %collective-permute-start.1 = (bf16[32,4096]{1,0:T(8,128)(2,1)S(1)}, bf16[32,4096]{1,0:T(8,128)(2,1)S(1)}, u32[]{:S(2)}, u32[]{:S(2)}) collective-permute-start(bf16[32,4096]{1,0:T(8,128)(2,1)S(1)} %copy-done.6), channel_id=1, source_target_pairs={{0,3},{1,0},{2,1},{3,2},{4,7},{5,4},{6,5},{7,6},{8,11},{9,8},{10,9... | collective-permute-start | bytes 786440 | tf_op jit(solution)/shard_map/ppermute | solution.py:189
  23.8 16.0 %collective-permute-start = (bf16[32,4096]{1,0:T(8,128)(2,1)S(1)}, bf16[32,4096]{1,0:T(8,128)(2,1)S(1)}, u32[]{:S(2)}, u32[]{:S(2)}) collective-permute-start(bf16[32,4096]{1,0:T(8,128)(2,1)S(1)} %copy-done.6), channel_id=1, source_target_pairs={{0,1},{1,2},{2,3},{3,0},{4,5},{5,6},{6,7},{7,4},{8,9},{9,10},{10,1... | collective-permute-start | bytes 786440 | tf_op jit(solution)/shard_map/ppermute | solution.py:185
  23.8 16.1 %collective-permute-start.2 = (bf16[32,4096]{1,0:T(8,128)(2,1)S(1)}, bf16[32,4096]{1,0:T(8,128)(2,1)S(1)}, u32[]{:S(2)}, u32[]{:S(2)}) collective-permute-start(bf16[32,4096]{1,0:T(8,128)(2,1)S(1)} %copy-done.6), channel_id=1, source_target_pairs={{0,2},{1,3},{2,0},{3,1},{4,6},{5,7},{6,4},{7,5},{8,10},{9,11},{10,... | collective-permute-start | bytes 786440 | tf_op jit(solution)/shard_map/ppermute | solution.py:193
  62.6 70.6 %all-to-all-start.1 = ((bf16[64,4,4096]{2,1,0:T(4,128)(2,1)}), bf16[64,4,4096]{2,1,0:T(4,128)(2,1)S(1)}, u32[]{:S(2)}, u32[]{:S(2)}) async-start(bf16[64,4,4096]{2,1,0:T(4,128)(2,1)} %reshape.34), calls=%async_computation.1 | async-start | bytes 4194304 | tf_op jit(solution)/shard_map/all_to_all | solution.py:331
  69.4 30.8 %copy-start = (bf16[64,8192]{1,0:T(8,128)(2,1)}, bf16[64,8192]{1,0:T(8,128)(2,1)S(1)}, u32[]{:S(2)}) copy-start(bf16[64,8192]{1,0:T(8,128)(2,1)S(1)} %slice.12.refs_0_.refs_5_) | copy-start | bytes 3145732
  69.4 25.6 %collective-permute-start.4 = (bf16[64,8192]{1,0:T(8,128)(2,1)S(1)}, bf16[64,8192]{1,0:T(8,128)(2,1)S(1)}, u32[]{:S(2)}, u32[]{:S(2)}) collective-permute-start(bf16[64,8192]{1,0:T(8,128)(2,1)S(1)} %slice.12.refs_0_.refs_5_), channel_id=1, source_target_pairs={{0,3},{1,0},{2,1},{3,2},{4,7},{5,4},{6,5},{7,6},{8,11},{9,8},{10,9... | collective-permute-start | bytes 3145736 | tf_op jit(solution)/shard_map/ppermute | solution.py:189
  72.2 26.5 %collective-permute-start.3 = (bf16[64,8192]{1,0:T(8,128)(2,1)S(1)}, bf16[64,8192]{1,0:T(8,128)(2,1)S(1)}, u32[]{:S(2)}, u32[]{:S(2)}) collective-permute-start(bf16[64,8192]{1,0:T(8,128)(2,1)S(1)} %slice.12.refs_0_.refs_5_), channel_id=1, source_target_pairs={{0,1},{1,2},{2,3},{3,0},{4,5},{5,6},{6,7},{7,4},{8,9},{9,10},{10,1... | collective-permute-start | bytes 3145736 | tf_op jit(solution)/shard_map/ppermute | solution.py:185
  95.0 14.4 %collective-permute-start.6 = (bf16[32,8192]{1,0:T(8,128)(2,1)S(1)}, bf16[32,8192]{1,0:T(8,128)(2,1)S(1)}, u32[]{:S(2)}, u32[]{:S(2)}) collective-permute-start(bf16[32,8192]{1,0:T(8,128)(2,1)S(1)} %slice.17), channel_id=1, source_target_pairs={{0,3},{1,0},{2,1},{3,2},{4,7},{5,4},{6,5},{7,6},{8,11},{9,8},{10,9... | collective-permute-start | bytes 1572872 | tf_op jit(solution)/shard_map/ppermute | solution.py:189
  98.8 14.3 %collective-permute-start.5 = (bf16[32,8192]{1,0:T(8,128)(2,1)S(1)}, bf16[32,8192]{1,0:T(8,128)(2,1)S(1)}, u32[]{:S(2)}, u32[]{:S(2)}) collective-permute-start(bf16[32,8192]{1,0:T(8,128)(2,1)S(1)} %slice.16), channel_id=1, source_target_pairs={{0,1},{1,2},{2,3},{3,0},{4,5},{5,6},{6,7},{7,4},{8,9},{9,10},{10,1... | collective-permute-start | bytes 1572872 | tf_op jit(solution)/shard_map/ppermute | solution.py:185
  100.2 26.5 %copy-start.5 = (bf16[64,4096]{1,0:T(8,128)(2,1)}, bf16[64,4096]{1,0:T(8,128)(2,1)S(1)}, u32[]{:S(2)}) copy-start(bf16[64,4096]{1,0:T(8,128)(2,1)S(1)} %slice.13.refs_0_) | copy-start | bytes 1572868
  113.1 16.7 %collective-permute-start.9 = (bf16[64,4096]{1,0:T(8,128)(2,1)S(1)}, bf16[64,4096]{1,0:T(8,128)(2,1)S(1)}, u32[]{:S(2)}, u32[]{:S(2)}) collective-permute-start(bf16[64,4096]{1,0:T(8,128)(2,1)S(1)} %slice.13.refs_0_), channel_id=1, source_target_pairs={{0,2},{1,3},{2,0},{3,1},{4,6},{5,7},{6,4},{7,5},{8,10},{9,11},{10,... | collective-permute-start | bytes 1572872 | tf_op jit(solution)/shard_map/ppermute | solution.py:193
  113.1 25.1 %collective-permute-start.8 = (bf16[64,4096]{1,0:T(8,128)(2,1)S(1)}, bf16[64,4096]{1,0:T(8,128)(2,1)}, u32[]{:S(2)}, u32[]{:S(2)}) collective-permute-start(bf16[64,4096]{1,0:T(8,128)(2,1)S(1)} %slice.13.refs_0_), channel_id=1, source_target_pairs={{0,3},{1,0},{2,1},{3,2},{4,7},{5,4},{6,5},{7,6},{8,11},{9,8},{10,9... | collective-permute-start | bytes 1572872 | tf_op jit(solution)/shard_map/ppermute | solution.py:189
  114.9 23.4 %collective-permute-start.7 = (bf16[64,4096]{1,0:T(8,128)(2,1)S(1)}, bf16[64,4096]{1,0:T(8,128)(2,1)}, u32[]{:S(2)}, u32[]{:S(2)}) collective-permute-start(bf16[64,4096]{1,0:T(8,128)(2,1)S(1)} %slice.13.refs_0_), channel_id=1, source_target_pairs={{0,1},{1,2},{2,3},{3,0},{4,5},{5,6},{6,7},{7,4},{8,9},{9,10},{10,1... | collective-permute-start | bytes 1572872 | tf_op jit(solution)/shard_map/ppermute | solution.py:185
  126.7 23.4 %collective-permute-start.10 = (bf16[64,4352]{1,0:T(8,128)(2,1)}, bf16[64,4352]{1,0:T(8,128)(2,1)S(1)}, u32[]{:S(2)}, u32[]{:S(2)}) collective-permute-start(bf16[64,4352]{1,0:T(8,128)(2,1)} %get-tuple-element.55), channel_id=1, source_target_pairs={{0,3},{1,0},{2,1},{3,2},{4,7},{5,4},{6,5},{7,6},{8,11},{9,8},{10,9... | collective-permute-start | bytes 1671176 | tf_op jit(solution)/shard_map/ppermute | solution.py:189
  129.8 22.9 %collective-permute-start.11 = (bf16[64,4352]{1,0:T(8,128)(2,1)}, bf16[64,4352]{1,0:T(8,128)(2,1)}, u32[]{:S(2)}, u32[]{:S(2)}) collective-permute-start(bf16[64,4352]{1,0:T(8,128)(2,1)} %get-tuple-element.56), channel_id=1, source_target_pairs={{0,1},{1,2},{2,3},{3,0},{4,5},{5,6},{6,7},{7,4},{8,9},{9,10},{10,1... | collective-permute-start | bytes 1671176 | tf_op jit(solution)/shard_map/ppermute | solution.py:185
  130.6 31.3 %collective-permute-start.12 = (bf16[64,4352]{1,0:T(8,128)(2,1)}, bf16[64,4352]{1,0:T(8,128)(2,1)}, u32[]{:S(2)}, u32[]{:S(2)}) collective-permute-start(bf16[64,4352]{1,0:T(8,128)(2,1)} %get-tuple-element.57), channel_id=1, source_target_pairs={{0,2},{1,3},{2,0},{3,1},{4,6},{5,7},{6,4},{7,5},{8,10},{9,11},{10,... | collective-permute-start | bytes 1671176 | tf_op jit(solution)/shard_map/ppermute | solution.py:193
  138.3 23.6 %copy-start.7 = (bf16[64,4352]{1,0:T(8,128)(2,1)S(1)}, bf16[64,4352]{1,0:T(8,128)(2,1)}, u32[]{:S(2)}) copy-start(bf16[64,4352]{1,0:T(8,128)(2,1)} %get-tuple-element.54) | copy-start | bytes 1671172
  163.3 25.5 %copy-start.8 = (bf16[64,4352]{1,0:T(8,128)(2,1)S(1)}, bf16[64,4352]{1,0:T(8,128)(2,1)}, u32[]{:S(2)}) copy-start(bf16[64,4352]{1,0:T(8,128)(2,1)} %get-tuple-element.68) | copy-start | bytes 1671172
  163.3 15.8 %collective-permute-start.13 = (bf16[64,4352]{1,0:T(8,128)(2,1)}, bf16[64,4352]{1,0:T(8,128)(2,1)S(1)}, u32[]{:S(2)}, u32[]{:S(2)}) collective-permute-start(bf16[64,4352]{1,0:T(8,128)(2,1)} %get-tuple-element.69), channel_id=1, source_target_pairs={{0,3},{1,0},{2,1},{3,2},{4,7},{5,4},{6,5},{7,6},{8,11},{9,8},{10,9... | collective-permute-start | bytes 1671176 | tf_op jit(solution)/shard_map/ppermute | solution.py:189
  163.8 25.1 %collective-permute-start.14 = (bf16[64,4352]{1,0:T(8,128)(2,1)}, bf16[64,4352]{1,0:T(8,128)(2,1)S(1)}, u32[]{:S(2)}, u32[]{:S(2)}) collective-permute-start(bf16[64,4352]{1,0:T(8,128)(2,1)} %get-tuple-element.70), channel_id=1, source_target_pairs={{0,1},{1,2},{2,3},{3,0},{4,5},{5,6},{6,7},{7,4},{8,9},{9,10},{10,1... | collective-permute-start | bytes 1671176 | tf_op jit(solution)/shard_map/ppermute | solution.py:185
  165.5 23.4 %collective-permute-start.15 = (bf16[64,4352]{1,0:T(8,128)(2,1)S(1)}, bf16[64,4352]{1,0:T(8,128)(2,1)S(1)}, u32[]{:S(2)}, u32[]{:S(2)}) collective-permute-start(bf16[64,4352]{1,0:T(8,128)(2,1)S(1)} %copy-done.16), channel_id=1, source_target_pairs={{0,2},{1,3},{2,0},{3,1},{4,6},{5,7},{6,4},{7,5},{8,10},{9,11},{10,... | collective-permute-start | bytes 1671176 | tf_op jit(solution)/shard_map/ppermute | solution.py:193
  166.7 28.6 %all-to-all-start.2 = ((bf16[64,2,2176]{2,1,0:T(2,128)(2,1)}), bf16[64,2,2176]{2,1,0:T(2,128)(2,1)S(1)}, u32[]{:S(2)}, u32[]{:S(2)}) async-start(bf16[64,2,2176]{2,1,0:T(2,128)(2,1)} %reshape.36), calls=%async_computation.2 | async-start | bytes 1114112 | tf_op jit(solution)/shard_map/all_to_all | solution.py:219
  195.2 24.1 %all-to-all-start.3 = ((bf16[64,2,2176]{2,1,0:T(2,128)(2,1)}), bf16[64,2,2176]{2,1,0:T(2,128)(2,1)S(1)}, u32[]{:S(2)}, u32[]{:S(2)}) async-start(bf16[64,2,2176]{2,1,0:T(2,128)(2,1)} %reshape.38), calls=%async_computation.3 | async-start | bytes 1114112 | tf_op jit(solution)/shard_map/all_to_all | solution.py:219
  (13 other events, 114.5 us)

commit v3 on v2

--- a/solution.py
+++ b/solution.py
@@ -10,7 +10,7 @@
 BF = jnp.bfloat16
 F32 = jnp.float32
 BLOCK = 128
-VMEM_MIB = 56
+VMEM_MIB = 44
 SPAN = 2048
 MIB = 1 << 20
 VMEM = pl.BlockSpec(memory_space=pltpu.VMEM)
@@ -197,8 +197,10 @@
     left, right = to_right(x, n), to_left(x, n)
     if direct:
         return [x, left, right, across(x, n)]
-    h = x.shape[0] // 2
-    return [x, left, right, to_right(left[:h], n), to_left(right[h:], n)]
+    h, q = x.shape[0] // 2, x.shape[0] // 4
+    first = [to_right(left[:q], n), to_left(right[h : h + q], n)]
+    second = [to_right(left[q:h], n), to_left(right[h + q :], n)]
+    return [x, left, right, first[0], second[0], first[1], second[1]]
 
 
 def home(terms, n):
@@ -326,7 +328,9 @@
         (exchange(send_a), send_d, both, back, down)
     )
     pieces_a = gather(rows_in[:, : 2 * width], n_tp, False)
-    rows_b, *pieces_a[3:] = lax.optimization_barrier((rows_in[:, 2 * width :], *pieces_a[3:]))
+    rows_b, pieces_a[3], pieces_a[5] = lax.optimization_barrier(
+        (rows_in[:, 2 * width :], pieces_a[3], pieces_a[5])
+    )
     pieces_b = gather(rows_b, n_tp, True)
     rows_d = lax.all_to_all(send_d, "ep", split_axis=0, concat_axis=0, tiled=True)
     rows_d = rows_d.reshape(experts, n_tp * width)

time: 225 us -> 213 us (0.947)
  waiting for transfers between devices: 97 us -> 87.9 us
  Pallas kernels: 43.6 us -> 40.4 us
    ppermute x6 -> x7, waiting for transfers between devices: 36.8 us -> 22.8 us  [to_left(): return lax.ppermute(v, 'tp', ring(n, -1))]
    ppermute x6 -> x7, waiting for transfers between devices: 16 us -> 27.1 us  [to_right(): return lax.ppermute(v, 'tp', ring(n, 1))]
    ppermute x4, waiting for transfers between devices: 9.14 us -> 0.01 us  [across(): return lax.ppermute(v, 'tp', ring(n, n // 2))]
    ppermute x6 -> x7, starting transfers between devices: 2.23 us -> 6.33 us  [to_right(): return lax.ppermute(v, 'tp', ring(n, 1))]
    all_to_all x3, waiting for transfers between devices: 35.1 us -> 38 us  [exchange(): lax.all_to_all(x.reshape(rows, 2, width // 2), 'ep', split_axis=0, concat...]
    ppermute x4, starting transfers between devices: 5.17 us -> 2.69 us  [across(): return lax.ppermute(v, 'tp', ring(n, n // 2))]
    ppermute x6 -> x7, starting transfers between devices: 14.6 us -> 12.7 us  [to_left(): return lax.ppermute(v, 'tp', ring(n, -1))]
  transfers between devices with their start and end apart: 20 -> 22, of which waited for: 12 -> 11; matrix products, arithmetic and copies ran while one was open for 7% -> 7% of each run, Pallas kernels for 17% -> 17%
where the time goes in v3:
time: 213 us; the launch traced here: 211 us
  waiting for transfers between devices  87.9 us (41%)
  starting transfers between devices  54 us (25%)
  Pallas kernels  40.4 us (19%)
  local copies, waits for them, and re-layouts  25.5 us (12%)
    all_to_all x3, waiting for transfers between devices, exchange(): lax.all_to_all(x.reshape(rows, 2, width // 2), 'ep', split_axis=0, concat...  38 us
    ppermute x7, waiting for transfers between devices, to_right(): return lax.ppermute(v, 'tp', ring(n, 1))  27.1 us
    all_to_all x3, starting transfers between devices, exchange(): lax.all_to_all(x.reshape(rows, 2, width // 2), 'ep', split_axis=0, concat...  26.7 us
    ppermute x7, waiting for transfers between devices, to_left(): return lax.ppermute(v, 'tp', ring(n, -1))  22.8 us
    pallas_call x2, Pallas kernels, products(): pl.pallas_call(functools.partial(expert_kernel, len(x_pieces), turns, len...  21.2 us
    ppermute x7, starting transfers between devices, to_left(): return lax.ppermute(v, 'tp', ring(n, -1))  12.7 us
    pallas_call x1, Pallas kernels, shards(): pl.pallas_call(prep_kernel, grid=(steps,), in_specs=[SMEM, SMEM, SMEM, pl...  11.8 us
    unnamed x39, local copies, waits for them, and re-layouts  7.63 us
  transfers between devices with their start and end apart: 22, of which 11 were waited for; matrix products, arithmetic and copies ran while one was open for 7% of the time, Pallas kernels for 17%

profile of v3, /device:TPU:8, one launch (start us, length us, event | category | flops | bytes accessed | tf_op | source)
XLA Modules:
  0.0 210.6 jit_solution(13907288302446272944)
XLA Ops:
  0.6 3.2 %pack.1 = (bf16[64,12288]{1,0:T(8,128)(2,1)}, bf16[32,128]{1,0:T(8,128)(2,1)}, bf16[3,128,32]{2,1,0:T(8,128)(2,1)}, bf16[4,64,32]{2,1,0:T(8,128)(2,1)}) custom-call(s32[1]{0:T(128)} %bitcast.t_ref, s32[3,128]{1,0:T(4,128)} %bitcast.37, bf16[3,128]{1,0:T(4,128)(2,1)} %bitcast.38, bf16[32,4096]{1,0:T(8,128)(2,1)} %x_ref.1, bf16[32,4096]{1,0:T(8,128)(2,1)} %refs_0_.1), custom_call_target="tpu_custom_call" | custom-call | flops 67108864 | bytes 3145728 | tf_op jit(solution)/shard_map/pack/pallas_call | solution.py:234
  3.8 4.9 %reshape.32 = bf16[64,2,6144]{2,1,0:T(2,128)(2,1)} reshape(bf16[64,12288]{1,0:T(8,128)(2,1)} %get-tuple-element.40) | data formatting | bytes 3145728 | tf_op jit(solution)/shard_map/reshape | solution.py:221
  8.7 12.2 %all-to-all-start = ((bf16[64,2,6144]{2,1,0:T(2,128)(2,1)}), bf16[64,2,6144]{2,1,0:T(2,128)(2,1)S(1)}, u32[]{:S(2)}, u32[]{:S(2)}) async-start(bf16[64,2,6144]{2,1,0:T(2,128)(2,1)} %reshape.32), calls=%async_computation | async-start | bytes 3145728 | tf_op jit(solution)/shard_map/all_to_all | solution.py:221
  21.0 2.8 %collective-permute-start.1 = (bf16[32,4096]{1,0:T(8,128)(2,1)S(1)}, bf16[32,4096]{1,0:T(8,128)(2,1)S(1)}, u32[]{:S(2)}, u32[]{:S(2)}) collective-permute-start(bf16[32,4096]{1,0:T(8,128)(2,1)S(1)} %copy-done.10), channel_id=1, source_target_pairs={{0,3},{1,0},{2,1},{3,2},{4,7},{5,4},{6,5},{7,6},{8,11},{9,8},{10,9... | collective-permute-start | bytes 786440 | tf_op jit(solution)/shard_map/ppermute | solution.py:189
  28.1 11.8 %prep.1 = (bf16[4096,768]{1,0:T(8,128)(2,1)}, bf16[768,4096]{1,0:T(8,128)(2,1)}, bf16[4096,384]{1,0:T(8,128)(2,1)}) custom-call(f32[32,3]{1,0:T(8,128)} %bitcast.34, f32[32,3]{1,0:T(8,128)} %bitcast.35, f32[3,32]{1,0:T(4,128)} %bitcast.36, bf16[4096,384]{1,0:T(8,128)(2,1)} %bitcast.29, bf16[4096,384]{1,0:T(8,128)(2,1)} %bitcast.30, bf16[384,4096]{1,0:T(8,128)(2,1)} %bitcast.31), custom_call_target="tpu_custom_call" | custom-call | flops 12582912 | bytes 25165824 | tf_op jit(solution)/shard_map/prep/pallas_call | solution.py:261
  40.8 3.2 %place.1 = bf16[64,16384]{1,0:T(8,128)(2,1)} custom-call(bf16[4,64,32]{2,1,0:T(8,128)(2,1)} %get-tuple-element.41.place_ref, bf16[32,4096]{1,0:T(8,128)(2,1)} %refs_0_.1, bf16[32,4096]{1,0:T(8,128)(2,1)} %copy-done.12, bf16[32,4096]{1,0:T(8,128)(2,1)} %copy-done.11, bf16[32,4096]{1,0:T(8,128)(2,1)} %copy-done.13), custom_call_target="tpu_custom_call" | custom-call | flops 67108864 | bytes 3145728 | tf_op jit(solution)/shard_map/place/pallas_call | solution.py:249
  44.0 4.5 %reshape.34 = bf16[64,4,4096]{2,1,0:T(4,128)(2,1)} reshape(bf16[64,16384]{1,0:T(8,128)(2,1)} %place.1) | data formatting | bytes 4194304 | tf_op jit(solution)/shard_map/reshape | solution.py:326
  48.5 12.5 %all-to-all-done = bf16[64,2,6144]{2,1,0:T(2,128)(2,1)S(1)} async-done(((bf16[64,2,6144]{2,1,0:T(2,128)(2,1)}), bf16[64,2,6144]{2,1,0:T(2,128)(2,1)S(1)}, u32[]{:S(2)}, u32[]{:S(2)}) %all-to-all-start) | async-done | bytes 1572896 | tf_op jit(solution)/shard_map/all_to_all | solution.py:221
  66.5 5.6 %all-to-all-start.1 = ((bf16[64,4,4096]{2,1,0:T(4,128)(2,1)}), bf16[64,4,4096]{2,1,0:T(4,128)(2,1)}, u32[]{:S(2)}, u32[]{:S(2)}) async-start(bf16[64,4,4096]{2,1,0:T(4,128)(2,1)} %reshape.34), calls=%async_computation.1 | async-start | bytes 4194304 | tf_op jit(solution)/shard_map/all_to_all | solution.py:335
  72.1 15.9 %collective-permute-done.4.refs_2_.refs_9_ = bf16[64,8192]{1,0:T(8,128)(2,1)} collective-permute-done((bf16[64,8192]{1,0:T(8,128)(2,1)}, bf16[64,8192]{1,0:T(8,128)(2,1)}, u32[]{:S(2)}, u32[]{:S(2)}) %collective-permute-start.4) | collective-permute-done | bytes 1048608 | tf_op jit(solution)/shard_map/ppermute | solution.py:189
  89.1 3.8 %collective-permute-start.6 = (bf16[16,8192]{1,0:T(8,128)(2,1)S(1)}, bf16[16,8192]{1,0:T(8,128)(2,1)S(1)}, u32[]{:S(2)}, u32[]{:S(2)}) collective-permute-start(bf16[16,8192]{1,0:T(8,128)(2,1)S(1)} %get-tuple-element.75), channel_id=1, source_target_pairs={{0,3},{1,0},{2,1},{3,2},{4,7},{5,4},{6,5},{7,6},{8,11},{9,8},{10,9... | collective-permute-start | bytes 786440 | tf_op jit(solution)/shard_map/ppermute | solution.py:189
  94.2 3.2 %collective-permute-start.8 = (bf16[16,8192]{1,0:T(8,128)(2,1)S(1)}, bf16[16,8192]{1,0:T(8,128)(2,1)S(1)}, u32[]{:S(2)}, u32[]{:S(2)}) collective-permute-start(bf16[16,8192]{1,0:T(8,128)(2,1)S(1)} %get-tuple-element.74), channel_id=1, source_target_pairs={{0,3},{1,0},{2,1},{3,2},{4,7},{5,4},{6,5},{7,6},{8,11},{9,8},{10,9... | collective-permute-start | bytes 786440 | tf_op jit(solution)/shard_map/ppermute | solution.py:189
  99.3 7.2 %collective-permute-done.5.refs_3_.refs_10_ = bf16[16,8192]{1,0:T(8,128)(2,1)S(1)} collective-permute-done((bf16[16,8192]{1,0:T(8,128)(2,1)S(1)}, bf16[16,8192]{1,0:T(8,128)(2,1)S(1)}, u32[]{:S(2)}, u32[]{:S(2)}) %collective-permute-start.5) | collective-permute-done | bytes 262176 | tf_op jit(solution)/shard_map/ppermute | solution.py:185
  108.6 3.8 %collective-permute-done.8.refs_6_.refs_13_ = bf16[16,8192]{1,0:T(8,128)(2,1)S(1)} collective-permute-done((bf16[16,8192]{1,0:T(8,128)(2,1)S(1)}, bf16[16,8192]{1,0:T(8,128)(2,1)S(1)}, u32[]{:S(2)}, u32[]{:S(2)}) %collective-permute-start.8) | collective-permute-done | bytes 262176 | tf_op jit(solution)/shard_map/ppermute | solution.py:189
  112.4 7.2 %collective-permute-done.7.refs_4_.refs_11_ = bf16[16,8192]{1,0:T(8,128)(2,1)S(1)} collective-permute-done((bf16[16,8192]{1,0:T(8,128)(2,1)S(1)}, bf16[16,8192]{1,0:T(8,128)(2,1)S(1)}, u32[]{:S(2)}, u32[]{:S(2)}) %collective-permute-start.7) | collective-permute-done | bytes 262176 | tf_op jit(solution)/shard_map/ppermute | solution.py:185
  119.6 10.7 %products.2 = (bf16[64,4352]{1,0:T(8,128)(2,1)S(1)}, bf16[64,4352]{1,0:T(8,128)(2,1)}, bf16[64,4352]{1,0:T(8,128)(2,1)}, bf16[64,4352]{1,0:T(8,128)(2,1)}) custom-call(bf16[64,8192]{1,0:T(8,128)(2,1)} %slice.18.refs_0_.refs_7_, bf16[64,8192]{1,0:T(8,128)(2,1)} %collective-permute-done.3.refs_1_.refs_8_, ...), custom_call_target="tpu_custom_call" | custom-call | flops 4026531840 | bytes 22020096 | tf_op jit(solution)/shard_map/products/pallas_call | solution.py:301
  133.9 2.9 %copy.18 = bf16[8,8,4,4096]{3,1,2,0:T(8,128)(2,1)S(1)} copy(bf16[8,8,4,4096]{3,2,1,0:T(4,128)(2,1)} %bitcast.12) | data formatting | bytes 4194304
  136.8 10.5 %products.3 = (bf16[64,4352]{1,0:T(8,128)(2,1)S(1)}, bf16[64,4352]{1,0:T(8,128)(2,1)}, bf16[64,4352]{1,0:T(8,128)(2,1)}, bf16[64,4352]{1,0:T(8,128)(2,1)}) custom-call(bf16[64,4096]{1,0:T(8,128)(2,1)} %slice.19.refs_0_, bf16[64,4096]{1,0:T(8,128)(2,1)} %collective-permute-done.9.refs_1_, bf16[64,4096]{1,0:T(8,128)(2,1)} %collective-permute-done.10.refs_2_, ...), custom_call_target="tpu_custom_call" | custom-call | flops 4026531840 | bytes 22020096 | tf_op jit(solution)/shard_map/products/pallas_call | solution.py:301
  149.1 4.3 %collective-permute-done.13 = bf16[64,4352]{1,0:T(8,128)(2,1)} collective-permute-done((bf16[64,4352]{1,0:T(8,128)(2,1)}, bf16[64,4352]{1,0:T(8,128)(2,1)}, u32[]{:S(2)}, u32[]{:S(2)}) %collective-permute-start.13) | collective-permute-done | bytes 557088 | tf_op jit(solution)/shard_map/ppermute | solution.py:185
  158.5 8.6 %all-to-all-start.2 = ((bf16[64,2,2176]{2,1,0:T(2,128)(2,1)}), bf16[64,2,2176]{2,1,0:T(2,128)(2,1)S(1)}, u32[]{:S(2)}, u32[]{:S(2)}) async-start(bf16[64,2,2176]{2,1,0:T(2,128)(2,1)} %reshape.36), calls=%async_computation.2 | async-start | bytes 1114112 | tf_op jit(solution)/shard_map/all_to_all | solution.py:221
  168.4 8.4 %collective-permute-done.16 = bf16[64,4352]{1,0:T(8,128)(2,1)S(1)} collective-permute-done((bf16[64,4352]{1,0:T(8,128)(2,1)}, bf16[64,4352]{1,0:T(8,128)(2,1)S(1)}, u32[]{:S(2)}, u32[]{:S(2)}) %collective-permute-start.16) | collective-permute-done | bytes 557088 | tf_op jit(solution)/shard_map/ppermute | solution.py:185
  178.1 7.3 %all-to-all-done.2 = bf16[64,2,2176]{2,1,0:T(2,128)(2,1)S(1)} async-done(((bf16[64,2,2176]{2,1,0:T(2,128)(2,1)}), bf16[64,2,2176]{2,1,0:T(2,128)(2,1)S(1)}, u32[]{:S(2)}, u32[]{:S(2)}) %all-to-all-start.2) | async-done | bytes 557088 | tf_op jit(solution)/shard_map/all_to_all | solution.py:221
  185.4 5.9 %all-to-all-start.3 = ((bf16[64,2,2176]{2,1,0:T(2,128)(2,1)}), bf16[64,2,2176]{2,1,0:T(2,128)(2,1)S(1)}, u32[]{:S(2)}, u32[]{:S(2)}) async-start(bf16[64,2,2176]{2,1,0:T(2,128)(2,1)} %reshape.38), calls=%async_computation.3 | async-start | bytes 1114112 | tf_op jit(solution)/shard_map/all_to_all | solution.py:221
  191.3 18.2 %all-to-all-done.3 = bf16[64,2,2176]{2,1,0:T(2,128)(2,1)S(1)} async-done(((bf16[64,2,2176]{2,1,0:T(2,128)(2,1)}), bf16[64,2,2176]{2,1,0:T(2,128)(2,1)S(1)}, u32[]{:S(2)}, u32[]{:S(2)}) %all-to-all-start.3) | async-done | bytes 557088 | tf_op jit(solution)/shard_map/all_to_all | solution.py:221
  (77 shorter events, 31.0 us)
Async XLA Ops:
  8.7 52.3 %all-to-all-start = ((bf16[64,2,6144]{2,1,0:T(2,128)(2,1)}), bf16[64,2,6144]{2,1,0:T(2,128)(2,1)S(1)}, u32[]{:S(2)}, u32[]{:S(2)}) async-start(bf16[64,2,6144]{2,1,0:T(2,128)(2,1)} %reshape.32), calls=%async_computation | async-start | bytes 3145728 | tf_op jit(solution)/shard_map/all_to_all | solution.py:221
  21.0 18.9 %collective-permute-start.1 = (bf16[32,4096]{1,0:T(8,128)(2,1)S(1)}, bf16[32,4096]{1,0:T(8,128)(2,1)S(1)}, u32[]{:S(2)}, u32[]{:S(2)}) collective-permute-start(bf16[32,4096]{1,0:T(8,128)(2,1)S(1)} %copy-done.10), channel_id=1, source_target_pairs={{0,3},{1,0},{2,1},{3,2},{4,7},{5,4},{6,5},{7,6},{8,11},{9,8},{10,9... | collective-permute-start | bytes 786440 | tf_op jit(solution)/shard_map/ppermute | solution.py:189
  23.8 16.1 %collective-permute-start = (bf16[32,4096]{1,0:T(8,128)(2,1)S(1)}, bf16[32,4096]{1,0:T(8,128)(2,1)S(1)}, u32[]{:S(2)}, u32[]{:S(2)}) collective-permute-start(bf16[32,4096]{1,0:T(8,128)(2,1)S(1)} %copy-done.10), channel_id=1, source_target_pairs={{0,1},{1,2},{2,3},{3,0},{4,5},{5,6},{6,7},{7,4},{8,9},{9,10},{10,1... | collective-permute-start | bytes 786440 | tf_op jit(solution)/shard_map/ppermute | solution.py:185
  23.8 16.1 %collective-permute-start.2 = (bf16[32,4096]{1,0:T(8,128)(2,1)S(1)}, bf16[32,4096]{1,0:T(8,128)(2,1)S(1)}, u32[]{:S(2)}, u32[]{:S(2)}) collective-permute-start(bf16[32,4096]{1,0:T(8,128)(2,1)S(1)} %copy-done.10), channel_id=1, source_target_pairs={{0,2},{1,3},{2,0},{3,1},{4,6},{5,7},{6,4},{7,5},{8,10},{9,11},{10,... | collective-permute-start | bytes 786440 | tf_op jit(solution)/shard_map/ppermute | solution.py:193
  63.7 24.3 %collective-permute-start.4 = (bf16[64,8192]{1,0:T(8,128)(2,1)}, bf16[64,8192]{1,0:T(8,128)(2,1)}, u32[]{:S(2)}, u32[]{:S(2)}) collective-permute-start(bf16[64,8192]{1,0:T(8,128)(2,1)} %slice.18.refs_0_.refs_7_), channel_id=1, source_target_pairs={{0,3},{1,0},{2,1},{3,2},{4,7},{5,4},{6,5},{7,6},{8,11},{9,8},{10,9... | collective-permute-start | bytes 3145736 | tf_op jit(solution)/shard_map/ppermute | solution.py:189
  66.5 26.4 %collective-permute-start.3 = (bf16[64,8192]{1,0:T(8,128)(2,1)}, bf16[64,8192]{1,0:T(8,128)(2,1)}, u32[]{:S(2)}, u32[]{:S(2)}) collective-permute-start(bf16[64,8192]{1,0:T(8,128)(2,1)} %slice.18.refs_0_.refs_7_), channel_id=1, source_target_pairs={{0,1},{1,2},{2,3},{3,0},{4,5},{5,6},{6,7},{7,4},{8,9},{9,10},{10,1... | collective-permute-start | bytes 3145736 | tf_op jit(solution)/shard_map/ppermute | solution.py:185
  66.5 67.4 %all-to-all-start.1 = ((bf16[64,4,4096]{2,1,0:T(4,128)(2,1)}), bf16[64,4,4096]{2,1,0:T(4,128)(2,1)}, u32[]{:S(2)}, u32[]{:S(2)}) async-start(bf16[64,4,4096]{2,1,0:T(4,128)(2,1)} %reshape.34), calls=%async_computation.1 | async-start | bytes 4194304 | tf_op jit(solution)/shard_map/all_to_all | solution.py:335
  72.1 47.5 %copy-start = (bf16[4096,384]{1,0:T(8,128)(2,1)S(1)}, bf16[4096,384]{1,0:T(8,128)(2,1)}, u32[]{:S(2)}) copy-start(bf16[4096,384]{1,0:T(8,128)(2,1)} %get-tuple-element.49.refs_15_.refs_9_) | copy-start | bytes 9437188
  89.1 10.3 %collective-permute-start.6 = (bf16[16,8192]{1,0:T(8,128)(2,1)S(1)}, bf16[16,8192]{1,0:T(8,128)(2,1)S(1)}, u32[]{:S(2)}, u32[]{:S(2)}) collective-permute-start(bf16[16,8192]{1,0:T(8,128)(2,1)S(1)} %get-tuple-element.75), channel_id=1, source_target_pairs={{0,3},{1,0},{2,1},{3,2},{4,7},{5,4},{6,5},{7,6},{8,11},{9,8},{10,9... | collective-permute-start | bytes 786440 | tf_op jit(solution)/shard_map/ppermute | solution.py:189
  93.9 12.6 %collective-permute-start.5 = (bf16[16,8192]{1,0:T(8,128)(2,1)S(1)}, bf16[16,8192]{1,0:T(8,128)(2,1)S(1)}, u32[]{:S(2)}, u32[]{:S(2)}) collective-permute-start(bf16[16,8192]{1,0:T(8,128)(2,1)S(1)} %get-tuple-element.77), channel_id=1, source_target_pairs={{0,1},{1,2},{2,3},{3,0},{4,5},{5,6},{6,7},{7,4},{8,9},{9,10},{10,1... | collective-permute-start | bytes 786440 | tf_op jit(solution)/shard_map/ppermute | solution.py:185
  94.2 18.2 %collective-permute-start.8 = (bf16[16,8192]{1,0:T(8,128)(2,1)S(1)}, bf16[16,8192]{1,0:T(8,128)(2,1)S(1)}, u32[]{:S(2)}, u32[]{:S(2)}) collective-permute-start(bf16[16,8192]{1,0:T(8,128)(2,1)S(1)} %get-tuple-element.74), channel_id=1, source_target_pairs={{0,3},{1,0},{2,1},{3,2},{4,7},{5,4},{6,5},{7,6},{8,11},{9,8},{10,9... | collective-permute-start | bytes 786440 | tf_op jit(solution)/shard_map/ppermute | solution.py:189
  97.4 22.2 %collective-permute-start.7 = (bf16[16,8192]{1,0:T(8,128)(2,1)S(1)}, bf16[16,8192]{1,0:T(8,128)(2,1)S(1)}, u32[]{:S(2)}, u32[]{:S(2)}) collective-permute-start(bf16[16,8192]{1,0:T(8,128)(2,1)S(1)} %get-tuple-element.76), channel_id=1, source_target_pairs={{0,1},{1,2},{2,3},{3,0},{4,5},{5,6},{6,7},{7,4},{8,9},{9,10},{10,1... | collective-permute-start | bytes 786440 | tf_op jit(solution)/shard_map/ppermute | solution.py:185
  106.5 26.6 %collective-permute-start.11 = (bf16[64,4096]{1,0:T(8,128)(2,1)}, bf16[64,4096]{1,0:T(8,128)(2,1)S(1)}, u32[]{:S(2)}, u32[]{:S(2)}) collective-permute-start(bf16[64,4096]{1,0:T(8,128)(2,1)} %slice.19.refs_0_), channel_id=1, source_target_pairs={{0,2},{1,3},{2,0},{3,1},{4,6},{5,7},{6,4},{7,5},{8,10},{9,11},{10,... | collective-permute-start | bytes 1572872 | tf_op jit(solution)/shard_map/ppermute | solution.py:193
  106.5 30.3 %collective-permute-start.10 = (bf16[64,4096]{1,0:T(8,128)(2,1)}, bf16[64,4096]{1,0:T(8,128)(2,1)}, u32[]{:S(2)}, u32[]{:S(2)}) collective-permute-start(bf16[64,4096]{1,0:T(8,128)(2,1)} %slice.19.refs_0_), channel_id=1, source_target_pairs={{0,3},{1,0},{2,1},{3,2},{4,7},{5,4},{6,5},{7,6},{8,11},{9,8},{10,9... | collective-permute-start | bytes 1572872 | tf_op jit(solution)/shard_map/ppermute | solution.py:189
  106.5 30.3 %collective-permute-start.9 = (bf16[64,4096]{1,0:T(8,128)(2,1)}, bf16[64,4096]{1,0:T(8,128)(2,1)}, u32[]{:S(2)}, u32[]{:S(2)}) collective-permute-start(bf16[64,4096]{1,0:T(8,128)(2,1)} %slice.19.refs_0_), channel_id=1, source_target_pairs={{0,1},{1,2},{2,3},{3,0},{4,5},{5,6},{6,7},{7,4},{8,9},{9,10},{10,1... | collective-permute-start | bytes 1572872 | tf_op jit(solution)/shard_map/ppermute | solution.py:185
  131.1 18.0 %collective-permute-start.12 = (bf16[64,4352]{1,0:T(8,128)(2,1)}, bf16[64,4352]{1,0:T(8,128)(2,1)}, u32[]{:S(2)}, u32[]{:S(2)}) collective-permute-start(bf16[64,4352]{1,0:T(8,128)(2,1)} %get-tuple-element.55), channel_id=1, source_target_pairs={{0,3},{1,0},{2,1},{3,2},{4,7},{5,4},{6,5},{7,6},{8,11},{9,8},{10,9... | collective-permute-start | bytes 1671176 | tf_op jit(solution)/shard_map/ppermute | solution.py:189
  131.1 22.3 %collective-permute-start.13 = (bf16[64,4352]{1,0:T(8,128)(2,1)}, bf16[64,4352]{1,0:T(8,128)(2,1)}, u32[]{:S(2)}, u32[]{:S(2)}) collective-permute-start(bf16[64,4352]{1,0:T(8,128)(2,1)} %get-tuple-element.56), channel_id=1, source_target_pairs={{0,1},{1,2},{2,3},{3,0},{4,5},{5,6},{6,7},{7,4},{8,9},{9,10},{10,1... | collective-permute-start | bytes 1671176 | tf_op jit(solution)/shard_map/ppermute | solution.py:185
  133.9 19.5 %collective-permute-start.14 = (bf16[64,4352]{1,0:T(8,128)(2,1)}, bf16[64,4352]{1,0:T(8,128)(2,1)}, u32[]{:S(2)}, u32[]{:S(2)}) collective-permute-start(bf16[64,4352]{1,0:T(8,128)(2,1)} %get-tuple-element.57), channel_id=1, source_target_pairs={{0,2},{1,3},{2,0},{3,1},{4,6},{5,7},{6,4},{7,5},{8,10},{9,11},{10,... | collective-permute-start | bytes 1671176 | tf_op jit(solution)/shard_map/ppermute | solution.py:193
  155.1 13.4 %collective-permute-start.15 = (bf16[64,4352]{1,0:T(8,128)(2,1)}, bf16[64,4352]{1,0:T(8,128)(2,1)S(1)}, u32[]{:S(2)}, u32[]{:S(2)}) collective-permute-start(bf16[64,4352]{1,0:T(8,128)(2,1)} %get-tuple-element.69), channel_id=1, source_target_pairs={{0,3},{1,0},{2,1},{3,2},{4,7},{5,4},{6,5},{7,6},{8,11},{9,8},{10,9... | collective-permute-start | bytes 1671176 | tf_op jit(solution)/shard_map/ppermute | solution.py:189
  155.2 21.7 %collective-permute-start.16 = (bf16[64,4352]{1,0:T(8,128)(2,1)}, bf16[64,4352]{1,0:T(8,128)(2,1)S(1)}, u32[]{:S(2)}, u32[]{:S(2)}) collective-permute-start(bf16[64,4352]{1,0:T(8,128)(2,1)} %get-tuple-element.70), channel_id=1, source_target_pairs={{0,1},{1,2},{2,3},{3,0},{4,5},{5,6},{6,7},{7,4},{8,9},{9,10},{10,1... | collective-permute-start | bytes 1671176 | tf_op jit(solution)/shard_map/ppermute | solution.py:185
  157.2 19.6 %collective-permute-start.17 = (bf16[64,4352]{1,0:T(8,128)(2,1)}, bf16[64,4352]{1,0:T(8,128)(2,1)S(1)}, u32[]{:S(2)}, u32[]{:S(2)}) collective-permute-start(bf16[64,4352]{1,0:T(8,128)(2,1)} %get-tuple-element.71), channel_id=1, source_target_pairs={{0,2},{1,3},{2,0},{3,1},{4,6},{5,7},{6,4},{7,5},{8,10},{9,11},{10,... | collective-permute-start | bytes 1671176 | tf_op jit(solution)/shard_map/ppermute | solution.py:193
  158.5 26.9 %all-to-all-start.2 = ((bf16[64,2,2176]{2,1,0:T(2,128)(2,1)}), bf16[64,2,2176]{2,1,0:T(2,128)(2,1)S(1)}, u32[]{:S(2)}, u32[]{:S(2)}) async-start(bf16[64,2,2176]{2,1,0:T(2,128)(2,1)} %reshape.36), calls=%async_computation.2 | async-start | bytes 1114112 | tf_op jit(solution)/shard_map/all_to_all | solution.py:221
  178.1 31.5 %copy-start.8 = (bf16[32,128]{1,0:T(8,128)(2,1)S(1)}, bf16[32,128]{1,0:T(8,128)(2,1)}, u32[]{:S(2)}) copy-start(bf16[32,128]{1,0:T(8,128)(2,1)} %get-tuple-element.38.comb_ref) | copy-start | bytes 24580
  185.4 24.1 %all-to-all-start.3 = ((bf16[64,2,2176]{2,1,0:T(2,128)(2,1)}), bf16[64,2,2176]{2,1,0:T(2,128)(2,1)S(1)}, u32[]{:S(2)}, u32[]{:S(2)}) async-start(bf16[64,2,2176]{2,1,0:T(2,128)(2,1)} %reshape.38), calls=%async_computation.3 | async-start | bytes 1114112 | tf_op jit(solution)/shard_map/all_to_all | solution.py:221
  (15 other events, 151.8 us)

commit v4 on v3

--- a/solution.py
+++ b/solution.py
@@ -66,11 +66,16 @@
         place_ref[q] = dot(every[experts:], keep(lax.rem(t + off, quarters))).astype(BF)
     send = dot(every, mine).astype(BF)
     step = 1024
+    half = sa_ref.shape[2]
+
+    def put(at, value):
+        sa_ref[:, at // half, at % half : at % half + step] = value
+
     for c in range(0, width, step):
         moved = dot(send, x_ref[:, c : c + step]).astype(BF)
-        sa_ref[:, c : c + step] = moved[:experts]
-        sa_ref[:, 2 * width + c : 2 * width + c + step] = moved[experts:]
-        sa_ref[:, width + c : width + c + step] = dot(send[:experts], d_ref[:, c : c + step]).astype(BF)
+        put(c, moved[:experts])
+        put(2 * width + c, moved[experts:])
+        put(width + c, dot(send[:experts], d_ref[:, c : c + step]).astype(BF))
 
 
 def place_kernel(place_ref, *refs):
@@ -236,7 +241,7 @@
         in_specs=[SMEM, VMEM, VMEM, VMEM, VMEM],
         out_specs=[VMEM] * 4,
         out_shape=[
-            jax.ShapeDtypeStruct((experts, 3 * width), BF),
+            jax.ShapeDtypeStruct((experts, 2, 3 * width // 2), BF),
             jax.ShapeDtypeStruct((rows, slots), BF),
             jax.ShapeDtypeStruct((top, slots, rows), BF),
             jax.ShapeDtypeStruct((n_tp, experts, rows), BF),
@@ -324,8 +329,10 @@
         )(*[array for array, _ in pieces], both, down, back)
 
     send_d = send_d.reshape(experts, n_tp, width)
+    rows_in = lax.all_to_all(send_a, "ep", split_axis=0, concat_axis=0, tiled=True)
+    rows_in = rows_in.reshape(experts, 3 * width)
     rows_in, send_d, both, back, down = lax.optimization_barrier(
-        (exchange(send_a), send_d, both, back, down)
+        (rows_in, send_d, both, back, down)
     )
     pieces_a = gather(rows_in[:, : 2 * width], n_tp, False)
     rows_b, pieces_a[3], pieces_a[5] = lax.optimization_barrier(

time: 213 us -> 208 us (0.977)
  local copies, waits for them, and re-layouts: 25.5 us -> 20.7 us
    all_to_all x3 -> x2, starting transfers between devices: 26.7 us -> 13.7 us  [exchange(): lax.all_to_all(x.reshape(rows, 2, width // 2), 'ep', split_axis=0, concat...]
    all_to_all x3 -> x2, waiting for transfers between devices: 38 us -> 25.5 us  [exchange(): lax.all_to_all(x.reshape(rows, 2, width // 2), 'ep', split_axis=0, concat...]
    all_to_all x0 -> x1, waiting for transfers between devices: none -> 12.5 us  [shards(): lax.all_to_all(send_a, 'ep', split_axis=0, concat_axis=0, tiled=True)]
    all_to_all x0 -> x1, starting transfers between devices: none -> 12.2 us  [shards(): lax.all_to_all(send_a, 'ep', split_axis=0, concat_axis=0, tiled=True)]
    ppermute x7, waiting for transfers between devices: 27.1 us -> 19.7 us  [to_right(): return lax.ppermute(v, 'tp', ring(n, 1))]
    ppermute x7, waiting for transfers between devices: 22.8 us -> 29.6 us  [to_left(): return lax.ppermute(v, 'tp', ring(n, -1))]
    reshape x3 -> x2, local copies, waits for them, and re-layouts: 6.78 us -> 1.89 us  [exchange(): x.reshape(rows, 2, width // 2)]
  transfers between devices with their start and end apart: 22 -> 22, of which waited for: 11 -> 12; matrix products, arithmetic and copies ran while one was open for 7% -> 8% of each run, Pallas kernels for 17% -> 18%
where the time goes in v4:
time: 208 us; the launch traced here: 206 us
  waiting for transfers between devices  88.6 us (43%)
  starting transfers between devices  53.1 us (26%)
  Pallas kernels  40.6 us (20%)
  local copies, waits for them, and re-layouts  20.7 us (10%)
    ppermute x7, waiting for transfers between devices, to_left(): return lax.ppermute(v, 'tp', ring(n, -1))  29.6 us
    all_to_all x2, waiting for transfers between devices, exchange(): lax.all_to_all(x.reshape(rows, 2, width // 2), 'ep', split_axis=0, concat...  25.5 us
    pallas_call x2, Pallas kernels, products(): pl.pallas_call(functools.partial(expert_kernel, len(x_pieces), turns, len...  21.2 us
    ppermute x7, waiting for transfers between devices, to_right(): return lax.ppermute(v, 'tp', ring(n, 1))  19.7 us
    all_to_all x2, starting transfers between devices, exchange(): lax.all_to_all(x.reshape(rows, 2, width // 2), 'ep', split_axis=0, concat...  13.7 us
    ppermute x7, starting transfers between devices, to_left(): return lax.ppermute(v, 'tp', ring(n, -1))  12.8 us
    all_to_all x1, waiting for transfers between devices, shards(): lax.all_to_all(send_a, 'ep', split_axis=0, concat_axis=0, tiled=True)  12.5 us
    all_to_all x1, starting transfers between devices, shards(): lax.all_to_all(send_a, 'ep', split_axis=0, concat_axis=0, tiled=True)  12.2 us
  transfers between devices with their start and end apart: 22, of which 12 were waited for; matrix products, arithmetic and copies ran while one was open for 8% of the time, Pallas kernels for 18%

profile of v4, /device:TPU:8, one launch (start us, length us, event | category | flops | bytes accessed | tf_op | source)
XLA Modules:
  0.0 205.9 jit_solution(7311292085838134526)
XLA Ops:
  0.6 3.4 %pack.1 = (bf16[64,2,6144]{2,1,0:T(2,128)(2,1)}, bf16[32,128]{1,0:T(8,128)(2,1)}, bf16[3,128,32]{2,1,0:T(8,128)(2,1)}, bf16[4,64,32]{2,1,0:T(8,128)(2,1)}) custom-call(s32[1]{0:T(128)} %bitcast.t_ref, s32[3,128]{1,0:T(4,128)} %bitcast.37, bf16[3,128]{1,0:T(4,128)(2,1)} %bitcast.38, bf16[32,4096]{1,0:T(8,128)(2,1)} %x_ref.1, bf16[32,4096]{1,0:T(8,128)(2,1)} %refs_0_.1), custom_call_target="tpu_custom_call" | custom-call | flops 67108864 | bytes 3145728 | tf_op jit(solution)/shard_map/pack/pallas_call | solution.py:239
  4.0 12.2 %all-to-all-start = ((bf16[64,2,6144]{2,1,0:T(2,128)(2,1)}), bf16[64,2,6144]{2,1,0:T(2,128)(2,1)S(1)}, u32[]{:S(2)}, u32[]{:S(2)}) async-start(bf16[64,2,6144]{2,1,0:T(2,128)(2,1)} %get-tuple-element.40), calls=%async_computation | async-start | bytes 3145728 | tf_op jit(solution)/shard_map/all_to_all | solution.py:332
  16.3 2.8 %collective-permute-start.1 = (bf16[32,4096]{1,0:T(8,128)(2,1)S(1)}, bf16[32,4096]{1,0:T(8,128)(2,1)S(1)}, u32[]{:S(2)}, u32[]{:S(2)}) collective-permute-start(bf16[32,4096]{1,0:T(8,128)(2,1)S(1)} %copy-done.10), channel_id=1, source_target_pairs={{0,3},{1,0},{2,1},{3,2},{4,7},{5,4},{6,5},{7,6},{8,11},{9,8},{10,9... | collective-permute-start | bytes 786440 | tf_op jit(solution)/shard_map/ppermute | solution.py:194
  23.4 11.8 %prep.1 = (bf16[4096,768]{1,0:T(8,128)(2,1)}, bf16[768,4096]{1,0:T(8,128)(2,1)}, bf16[4096,384]{1,0:T(8,128)(2,1)}) custom-call(f32[32,3]{1,0:T(8,128)} %bitcast.34, f32[32,3]{1,0:T(8,128)} %bitcast.35, f32[3,32]{1,0:T(4,128)} %bitcast.36, bf16[4096,384]{1,0:T(8,128)(2,1)} %bitcast.29, bf16[4096,384]{1,0:T(8,128)(2,1)} %bitcast.30, bf16[384,4096]{1,0:T(8,128)(2,1)} %bitcast.31), custom_call_target="tpu_custom_call" | custom-call | flops 12582912 | bytes 25165824 | tf_op jit(solution)/shard_map/prep/pallas_call | solution.py:266
  36.1 3.2 %place.1 = bf16[64,16384]{1,0:T(8,128)(2,1)} custom-call(bf16[4,64,32]{2,1,0:T(8,128)(2,1)} %get-tuple-element.41.place_ref, bf16[32,4096]{1,0:T(8,128)(2,1)} %refs_0_.1, bf16[32,4096]{1,0:T(8,128)(2,1)} %copy-done.12, bf16[32,4096]{1,0:T(8,128)(2,1)} %copy-done.11, bf16[32,4096]{1,0:T(8,128)(2,1)} %copy-done.13), custom_call_target="tpu_custom_call" | custom-call | flops 67108864 | bytes 3145728 | tf_op jit(solution)/shard_map/place/pallas_call | solution.py:254
  39.3 4.5 %reshape.30 = bf16[64,4,4096]{2,1,0:T(4,128)(2,1)} reshape(bf16[64,16384]{1,0:T(8,128)(2,1)} %place.1) | data formatting | bytes 4194304 | tf_op jit(solution)/shard_map/reshape | solution.py:331
  43.8 12.5 %all-to-all-done = bf16[64,2,6144]{2,1,0:T(2,128)(2,1)S(1)} async-done(((bf16[64,2,6144]{2,1,0:T(2,128)(2,1)}), bf16[64,2,6144]{2,1,0:T(2,128)(2,1)S(1)}, u32[]{:S(2)}, u32[]{:S(2)}) %all-to-all-start) | async-done | bytes 1572896 | tf_op jit(solution)/shard_map/all_to_all | solution.py:332
  61.8 5.6 %all-to-all-start.1 = ((bf16[64,4,4096]{2,1,0:T(4,128)(2,1)}), bf16[64,4,4096]{2,1,0:T(4,128)(2,1)}, u32[]{:S(2)}, u32[]{:S(2)}) async-start(bf16[64,4,4096]{2,1,0:T(4,128)(2,1)} %reshape.30), calls=%async_computation.1 | async-start | bytes 4194304 | tf_op jit(solution)/shard_map/all_to_all | solution.py:342
  67.4 15.9 %collective-permute-done.4.refs_2_.refs_9_ = bf16[64,8192]{1,0:T(8,128)(2,1)} collective-permute-done((bf16[64,8192]{1,0:T(8,128)(2,1)}, bf16[64,8192]{1,0:T(8,128)(2,1)}, u32[]{:S(2)}, u32[]{:S(2)}) %collective-permute-start.4) | collective-permute-done | bytes 1048608 | tf_op jit(solution)/shard_map/ppermute | solution.py:194
  84.5 3.8 %collective-permute-start.6 = (bf16[16,8192]{1,0:T(8,128)(2,1)S(1)}, bf16[16,8192]{1,0:T(8,128)(2,1)S(1)}, u32[]{:S(2)}, u32[]{:S(2)}) collective-permute-start(bf16[16,8192]{1,0:T(8,128)(2,1)S(1)} %get-tuple-element.75), channel_id=1, source_target_pairs={{0,3},{1,0},{2,1},{3,2},{4,7},{5,4},{6,5},{7,6},{8,11},{9,8},{10,9... | collective-permute-start | bytes 786440 | tf_op jit(solution)/shard_map/ppermute | solution.py:194
  89.5 3.2 %collective-permute-start.8 = (bf16[16,8192]{1,0:T(8,128)(2,1)S(1)}, bf16[16,8192]{1,0:T(8,128)(2,1)S(1)}, u32[]{:S(2)}, u32[]{:S(2)}) collective-permute-start(bf16[16,8192]{1,0:T(8,128)(2,1)S(1)} %get-tuple-element.74), channel_id=1, source_target_pairs={{0,3},{1,0},{2,1},{3,2},{4,7},{5,4},{6,5},{7,6},{8,11},{9,8},{10,9... | collective-permute-start | bytes 786440 | tf_op jit(solution)/shard_map/ppermute | solution.py:194
  94.6 7.2 %collective-permute-done.5.refs_3_.refs_10_ = bf16[16,8192]{1,0:T(8,128)(2,1)S(1)} collective-permute-done((bf16[16,8192]{1,0:T(8,128)(2,1)S(1)}, bf16[16,8192]{1,0:T(8,128)(2,1)S(1)}, u32[]{:S(2)}, u32[]{:S(2)}) %collective-permute-start.5) | collective-permute-done | bytes 262176 | tf_op jit(solution)/shard_map/ppermute | solution.py:190
  103.8 4.7 %collective-permute-done.8.refs_6_.refs_13_ = bf16[16,8192]{1,0:T(8,128)(2,1)S(1)} collective-permute-done((bf16[16,8192]{1,0:T(8,128)(2,1)S(1)}, bf16[16,8192]{1,0:T(8,128)(2,1)S(1)}, u32[]{:S(2)}, u32[]{:S(2)}) %collective-permute-start.8) | collective-permute-done | bytes 262176 | tf_op jit(solution)/shard_map/ppermute | solution.py:194
  108.5 6.4 %collective-permute-done.7.refs_4_.refs_11_ = bf16[16,8192]{1,0:T(8,128)(2,1)S(1)} collective-permute-done((bf16[16,8192]{1,0:T(8,128)(2,1)S(1)}, bf16[16,8192]{1,0:T(8,128)(2,1)S(1)}, u32[]{:S(2)}, u32[]{:S(2)}) %collective-permute-start.7) | collective-permute-done | bytes 262176 | tf_op jit(solution)/shard_map/ppermute | solution.py:190
  114.9 10.7 %products.2 = (bf16[64,4352]{1,0:T(8,128)(2,1)S(1)}, bf16[64,4352]{1,0:T(8,128)(2,1)}, bf16[64,4352]{1,0:T(8,128)(2,1)}, bf16[64,4352]{1,0:T(8,128)(2,1)}) custom-call(bf16[64,8192]{1,0:T(8,128)(2,1)} %slice.18.refs_0_.refs_7_, bf16[64,8192]{1,0:T(8,128)(2,1)} %collective-permute-done.3.refs_1_.refs_8_, ...), custom_call_target="tpu_custom_call" | custom-call | flops 4026531840 | bytes 22020096 | tf_op jit(solution)/shard_map/products/pallas_call | solution.py:306
  129.2 2.9 %copy.18 = bf16[8,8,4,4096]{3,1,2,0:T(8,128)(2,1)S(1)} copy(bf16[8,8,4,4096]{3,2,1,0:T(4,128)(2,1)} %bitcast.12) | data formatting | bytes 4194304
  132.2 10.5 %products.3 = (bf16[64,4352]{1,0:T(8,128)(2,1)S(1)}, bf16[64,4352]{1,0:T(8,128)(2,1)}, bf16[64,4352]{1,0:T(8,128)(2,1)}, bf16[64,4352]{1,0:T(8,128)(2,1)}) custom-call(bf16[64,4096]{1,0:T(8,128)(2,1)} %slice.19.refs_0_, bf16[64,4096]{1,0:T(8,128)(2,1)} %collective-permute-done.9.refs_1_, bf16[64,4096]{1,0:T(8,128)(2,1)} %collective-permute-done.10.refs_2_, ...), custom_call_target="tpu_custom_call" | custom-call | flops 4026531840 | bytes 22020096 | tf_op jit(solution)/shard_map/products/pallas_call | solution.py:306
  142.7 3.2 %collective-permute-done.12 = bf16[64,4352]{1,0:T(8,128)(2,1)} collective-permute-done((bf16[64,4352]{1,0:T(8,128)(2,1)}, bf16[64,4352]{1,0:T(8,128)(2,1)}, u32[]{:S(2)}, u32[]{:S(2)}) %collective-permute-start.12) | collective-permute-done | bytes 557088 | tf_op jit(solution)/shard_map/ppermute | solution.py:194
  154.6 7.8 %all-to-all-start.2 = ((bf16[64,2,2176]{2,1,0:T(2,128)(2,1)}), bf16[64,2,2176]{2,1,0:T(2,128)(2,1)S(1)}, u32[]{:S(2)}, u32[]{:S(2)}) async-start(bf16[64,2,2176]{2,1,0:T(2,128)(2,1)} %reshape.32), calls=%async_computation.2 | async-start | bytes 1114112 | tf_op jit(solution)/shard_map/all_to_all | solution.py:226
  162.4 5.8 %collective-permute-done.15 = bf16[64,4352]{1,0:T(8,128)(2,1)S(1)} collective-permute-done((bf16[64,4352]{1,0:T(8,128)(2,1)}, bf16[64,4352]{1,0:T(8,128)(2,1)S(1)}, u32[]{:S(2)}, u32[]{:S(2)}) %collective-permute-start.15) | collective-permute-done | bytes 557088 | tf_op jit(solution)/shard_map/ppermute | solution.py:194
  168.2 4.0 %collective-permute-done.16 = bf16[64,4352]{1,0:T(8,128)(2,1)S(1)} collective-permute-done((bf16[64,4352]{1,0:T(8,128)(2,1)}, bf16[64,4352]{1,0:T(8,128)(2,1)S(1)}, u32[]{:S(2)}, u32[]{:S(2)}) %collective-permute-start.16) | collective-permute-done | bytes 557088 | tf_op jit(solution)/shard_map/ppermute | solution.py:190
  173.4 7.3 %all-to-all-done.2 = bf16[64,2,2176]{2,1,0:T(2,128)(2,1)S(1)} async-done(((bf16[64,2,2176]{2,1,0:T(2,128)(2,1)}), bf16[64,2,2176]{2,1,0:T(2,128)(2,1)S(1)}, u32[]{:S(2)}, u32[]{:S(2)}) %all-to-all-start.2) | async-done | bytes 557088 | tf_op jit(solution)/shard_map/all_to_all | solution.py:226
  180.7 5.9 %all-to-all-start.3 = ((bf16[64,2,2176]{2,1,0:T(2,128)(2,1)}), bf16[64,2,2176]{2,1,0:T(2,128)(2,1)S(1)}, u32[]{:S(2)}, u32[]{:S(2)}) async-start(bf16[64,2,2176]{2,1,0:T(2,128)(2,1)} %reshape.34), calls=%async_computation.3 | async-start | bytes 1114112 | tf_op jit(solution)/shard_map/all_to_all | solution.py:226
  186.6 18.2 %all-to-all-done.3 = bf16[64,2,2176]{2,1,0:T(2,128)(2,1)S(1)} async-done(((bf16[64,2,2176]{2,1,0:T(2,128)(2,1)}), bf16[64,2,2176]{2,1,0:T(2,128)(2,1)S(1)}, u32[]{:S(2)}, u32[]{:S(2)}) %all-to-all-start.3) | async-done | bytes 557088 | tf_op jit(solution)/shard_map/all_to_all | solution.py:226
  (76 shorter events, 31.6 us)
Async XLA Ops:
  4.0 52.3 %all-to-all-start = ((bf16[64,2,6144]{2,1,0:T(2,128)(2,1)}), bf16[64,2,6144]{2,1,0:T(2,128)(2,1)S(1)}, u32[]{:S(2)}, u32[]{:S(2)}) async-start(bf16[64,2,6144]{2,1,0:T(2,128)(2,1)} %get-tuple-element.40), calls=%async_computation | async-start | bytes 3145728 | tf_op jit(solution)/shard_map/all_to_all | solution.py:332
  16.3 18.9 %collective-permute-start.1 = (bf16[32,4096]{1,0:T(8,128)(2,1)S(1)}, bf16[32,4096]{1,0:T(8,128)(2,1)S(1)}, u32[]{:S(2)}, u32[]{:S(2)}) collective-permute-start(bf16[32,4096]{1,0:T(8,128)(2,1)S(1)} %copy-done.10), channel_id=1, source_target_pairs={{0,3},{1,0},{2,1},{3,2},{4,7},{5,4},{6,5},{7,6},{8,11},{9,8},{10,9... | collective-permute-start | bytes 786440 | tf_op jit(solution)/shard_map/ppermute | solution.py:194
  19.1 16.1 %collective-permute-start = (bf16[32,4096]{1,0:T(8,128)(2,1)S(1)}, bf16[32,4096]{1,0:T(8,128)(2,1)S(1)}, u32[]{:S(2)}, u32[]{:S(2)}) collective-permute-start(bf16[32,4096]{1,0:T(8,128)(2,1)S(1)} %copy-done.10), channel_id=1, source_target_pairs={{0,1},{1,2},{2,3},{3,0},{4,5},{5,6},{6,7},{7,4},{8,9},{9,10},{10,1... | collective-permute-start | bytes 786440 | tf_op jit(solution)/shard_map/ppermute | solution.py:190
  19.1 16.1 %collective-permute-start.2 = (bf16[32,4096]{1,0:T(8,128)(2,1)S(1)}, bf16[32,4096]{1,0:T(8,128)(2,1)S(1)}, u32[]{:S(2)}, u32[]{:S(2)}) collective-permute-start(bf16[32,4096]{1,0:T(8,128)(2,1)S(1)} %copy-done.10), channel_id=1, source_target_pairs={{0,2},{1,3},{2,0},{3,1},{4,6},{5,7},{6,4},{7,5},{8,10},{9,11},{10,... | collective-permute-start | bytes 786440 | tf_op jit(solution)/shard_map/ppermute | solution.py:198
  59.0 24.3 %collective-permute-start.4 = (bf16[64,8192]{1,0:T(8,128)(2,1)}, bf16[64,8192]{1,0:T(8,128)(2,1)}, u32[]{:S(2)}, u32[]{:S(2)}) collective-permute-start(bf16[64,8192]{1,0:T(8,128)(2,1)} %slice.18.refs_0_.refs_7_), channel_id=1, source_target_pairs={{0,3},{1,0},{2,1},{3,2},{4,7},{5,4},{6,5},{7,6},{8,11},{9,8},{10,9... | collective-permute-start | bytes 3145736 | tf_op jit(solution)/shard_map/ppermute | solution.py:194
  61.8 26.5 %collective-permute-start.3 = (bf16[64,8192]{1,0:T(8,128)(2,1)}, bf16[64,8192]{1,0:T(8,128)(2,1)}, u32[]{:S(2)}, u32[]{:S(2)}) collective-permute-start(bf16[64,8192]{1,0:T(8,128)(2,1)} %slice.18.refs_0_.refs_7_), channel_id=1, source_target_pairs={{0,1},{1,2},{2,3},{3,0},{4,5},{5,6},{6,7},{7,4},{8,9},{9,10},{10,1... | collective-permute-start | bytes 3145736 | tf_op jit(solution)/shard_map/ppermute | solution.py:190
  61.8 67.4 %all-to-all-start.1 = ((bf16[64,4,4096]{2,1,0:T(4,128)(2,1)}), bf16[64,4,4096]{2,1,0:T(4,128)(2,1)}, u32[]{:S(2)}, u32[]{:S(2)}) async-start(bf16[64,4,4096]{2,1,0:T(4,128)(2,1)} %reshape.30), calls=%async_computation.1 | async-start | bytes 4194304 | tf_op jit(solution)/shard_map/all_to_all | solution.py:342
  83.3 31.6 %copy-start = (bf16[4096,384]{1,0:T(8,128)(2,1)S(1)}, bf16[4096,384]{1,0:T(8,128)(2,1)}, u32[]{:S(2)}) copy-start(bf16[4096,384]{1,0:T(8,128)(2,1)} %get-tuple-element.49.refs_15_.refs_9_) | copy-start | bytes 9437188
  84.5 10.1 %collective-permute-start.6 = (bf16[16,8192]{1,0:T(8,128)(2,1)S(1)}, bf16[16,8192]{1,0:T(8,128)(2,1)S(1)}, u32[]{:S(2)}, u32[]{:S(2)}) collective-permute-start(bf16[16,8192]{1,0:T(8,128)(2,1)S(1)} %get-tuple-element.75), channel_id=1, source_target_pairs={{0,3},{1,0},{2,1},{3,2},{4,7},{5,4},{6,5},{7,6},{8,11},{9,8},{10,9... | collective-permute-start | bytes 786440 | tf_op jit(solution)/shard_map/ppermute | solution.py:194
  89.4 12.4 %collective-permute-start.5 = (bf16[16,8192]{1,0:T(8,128)(2,1)S(1)}, bf16[16,8192]{1,0:T(8,128)(2,1)S(1)}, u32[]{:S(2)}, u32[]{:S(2)}) collective-permute-start(bf16[16,8192]{1,0:T(8,128)(2,1)S(1)} %get-tuple-element.77), channel_id=1, source_target_pairs={{0,1},{1,2},{2,3},{3,0},{4,5},{5,6},{6,7},{7,4},{8,9},{9,10},{10,1... | collective-permute-start | bytes 786440 | tf_op jit(solution)/shard_map/ppermute | solution.py:190
  89.5 19.1 %collective-permute-start.8 = (bf16[16,8192]{1,0:T(8,128)(2,1)S(1)}, bf16[16,8192]{1,0:T(8,128)(2,1)S(1)}, u32[]{:S(2)}, u32[]{:S(2)}) collective-permute-start(bf16[16,8192]{1,0:T(8,128)(2,1)S(1)} %get-tuple-element.74), channel_id=1, source_target_pairs={{0,3},{1,0},{2,1},{3,2},{4,7},{5,4},{6,5},{7,6},{8,11},{9,8},{10,9... | collective-permute-start | bytes 786440 | tf_op jit(solution)/shard_map/ppermute | solution.py:194
  92.7 22.2 %collective-permute-start.7 = (bf16[16,8192]{1,0:T(8,128)(2,1)S(1)}, bf16[16,8192]{1,0:T(8,128)(2,1)S(1)}, u32[]{:S(2)}, u32[]{:S(2)}) collective-permute-start(bf16[16,8192]{1,0:T(8,128)(2,1)S(1)} %get-tuple-element.76), channel_id=1, source_target_pairs={{0,1},{1,2},{2,3},{3,0},{4,5},{5,6},{6,7},{7,4},{8,9},{9,10},{10,1... | collective-permute-start | bytes 786440 | tf_op jit(solution)/shard_map/ppermute | solution.py:190
  101.8 26.7 %collective-permute-start.11 = (bf16[64,4096]{1,0:T(8,128)(2,1)}, bf16[64,4096]{1,0:T(8,128)(2,1)S(1)}, u32[]{:S(2)}, u32[]{:S(2)}) collective-permute-start(bf16[64,4096]{1,0:T(8,128)(2,1)} %slice.19.refs_0_), channel_id=1, source_target_pairs={{0,2},{1,3},{2,0},{3,1},{4,6},{5,7},{6,4},{7,5},{8,10},{9,11},{10,... | collective-permute-start | bytes 1572872 | tf_op jit(solution)/shard_map/ppermute | solution.py:198
  101.8 30.3 %collective-permute-start.10 = (bf16[64,4096]{1,0:T(8,128)(2,1)}, bf16[64,4096]{1,0:T(8,128)(2,1)}, u32[]{:S(2)}, u32[]{:S(2)}) collective-permute-start(bf16[64,4096]{1,0:T(8,128)(2,1)} %slice.19.refs_0_), channel_id=1, source_target_pairs={{0,3},{1,0},{2,1},{3,2},{4,7},{5,4},{6,5},{7,6},{8,11},{9,8},{10,9... | collective-permute-start | bytes 1572872 | tf_op jit(solution)/shard_map/ppermute | solution.py:194
  101.8 30.4 %collective-permute-start.9 = (bf16[64,4096]{1,0:T(8,128)(2,1)}, bf16[64,4096]{1,0:T(8,128)(2,1)}, u32[]{:S(2)}, u32[]{:S(2)}) collective-permute-start(bf16[64,4096]{1,0:T(8,128)(2,1)} %slice.19.refs_0_), channel_id=1, source_target_pairs={{0,1},{1,2},{2,3},{3,0},{4,5},{5,6},{6,7},{7,4},{8,9},{9,10},{10,1... | collective-permute-start | bytes 1572872 | tf_op jit(solution)/shard_map/ppermute | solution.py:190
  126.4 19.4 %collective-permute-start.12 = (bf16[64,4352]{1,0:T(8,128)(2,1)}, bf16[64,4352]{1,0:T(8,128)(2,1)}, u32[]{:S(2)}, u32[]{:S(2)}) collective-permute-start(bf16[64,4352]{1,0:T(8,128)(2,1)} %get-tuple-element.55), channel_id=1, source_target_pairs={{0,3},{1,0},{2,1},{3,2},{4,7},{5,4},{6,5},{7,6},{8,11},{9,8},{10,9... | collective-permute-start | bytes 1671176 | tf_op jit(solution)/shard_map/ppermute | solution.py:194
  126.4 21.6 %collective-permute-start.13 = (bf16[64,4352]{1,0:T(8,128)(2,1)}, bf16[64,4352]{1,0:T(8,128)(2,1)}, u32[]{:S(2)}, u32[]{:S(2)}) collective-permute-start(bf16[64,4352]{1,0:T(8,128)(2,1)} %get-tuple-element.56), channel_id=1, source_target_pairs={{0,1},{1,2},{2,3},{3,0},{4,5},{5,6},{6,7},{7,4},{8,9},{9,10},{10,1... | collective-permute-start | bytes 1671176 | tf_op jit(solution)/shard_map/ppermute | solution.py:190
  129.2 20.2 %collective-permute-start.14 = (bf16[64,4352]{1,0:T(8,128)(2,1)}, bf16[64,4352]{1,0:T(8,128)(2,1)}, u32[]{:S(2)}, u32[]{:S(2)}) collective-permute-start(bf16[64,4352]{1,0:T(8,128)(2,1)} %get-tuple-element.57), channel_id=1, source_target_pairs={{0,2},{1,3},{2,0},{3,1},{4,6},{5,7},{6,4},{7,5},{8,10},{9,11},{10,... | collective-permute-start | bytes 1671176 | tf_op jit(solution)/shard_map/ppermute | solution.py:198
  151.1 21.0 %copy-start.4 = (bf16[64,4352]{1,0:T(8,128)(2,1)S(1)}, bf16[64,4352]{1,0:T(8,128)(2,1)}, u32[]{:S(2)}) copy-start(bf16[64,4352]{1,0:T(8,128)(2,1)} %copy-done.3) | copy-start | bytes 1671172
  151.1 17.0 %collective-permute-start.15 = (bf16[64,4352]{1,0:T(8,128)(2,1)}, bf16[64,4352]{1,0:T(8,128)(2,1)S(1)}, u32[]{:S(2)}, u32[]{:S(2)}) collective-permute-start(bf16[64,4352]{1,0:T(8,128)(2,1)} %get-tuple-element.69), channel_id=1, source_target_pairs={{0,3},{1,0},{2,1},{3,2},{4,7},{5,4},{6,5},{7,6},{8,11},{9,8},{10,9... | collective-permute-start | bytes 1671176 | tf_op jit(solution)/shard_map/ppermute | solution.py:194
  151.3 20.8 %collective-permute-start.16 = (bf16[64,4352]{1,0:T(8,128)(2,1)}, bf16[64,4352]{1,0:T(8,128)(2,1)S(1)}, u32[]{:S(2)}, u32[]{:S(2)}) collective-permute-start(bf16[64,4352]{1,0:T(8,128)(2,1)} %get-tuple-element.70), channel_id=1, source_target_pairs={{0,1},{1,2},{2,3},{3,0},{4,5},{5,6},{6,7},{7,4},{8,9},{9,10},{10,1... | collective-permute-start | bytes 1671176 | tf_op jit(solution)/shard_map/ppermute | solution.py:190
  153.2 18.9 %collective-permute-start.17 = (bf16[64,4352]{1,0:T(8,128)(2,1)}, bf16[64,4352]{1,0:T(8,128)(2,1)S(1)}, u32[]{:S(2)}, u32[]{:S(2)}) collective-permute-start(bf16[64,4352]{1,0:T(8,128)(2,1)} %get-tuple-element.71), channel_id=1, source_target_pairs={{0,2},{1,3},{2,0},{3,1},{4,6},{5,7},{6,4},{7,5},{8,10},{9,11},{10,... | collective-permute-start | bytes 1671176 | tf_op jit(solution)/shard_map/ppermute | solution.py:198
  154.6 26.1 %all-to-all-start.2 = ((bf16[64,2,2176]{2,1,0:T(2,128)(2,1)}), bf16[64,2,2176]{2,1,0:T(2,128)(2,1)S(1)}, u32[]{:S(2)}, u32[]{:S(2)}) async-start(bf16[64,2,2176]{2,1,0:T(2,128)(2,1)} %reshape.32), calls=%async_computation.2 | async-start | bytes 1114112 | tf_op jit(solution)/shard_map/all_to_all | solution.py:226
  180.7 24.1 %all-to-all-start.3 = ((bf16[64,2,2176]{2,1,0:T(2,128)(2,1)}), bf16[64,2,2176]{2,1,0:T(2,128)(2,1)S(1)}, u32[]{:S(2)}, u32[]{:S(2)}) async-start(bf16[64,2,2176]{2,1,0:T(2,128)(2,1)} %reshape.34), calls=%async_computation.3 | async-start | bytes 1114112 | tf_op jit(solution)/shard_map/all_to_all | solution.py:226
  (15 other events, 136.8 us)
